TPU v7x, 1024 devices: a whole 4x8x16 slice. The times are simulated.
1024 devices in a mesh: dp: 128 (over y_hi, z, core), mp: 8 (over x, y_lo).
Axes of the slice: x: 4, y: 8 (y_hi: 4, y_lo: 2; y = y_hi * 2 + y_lo), z: 16, core: 2. Of those that a mesh axis runs over, the one named last changes fastest.
Arguments:
- image_feats: bfloat16 [40960, 1152], P('dp'), may hold values from -4 to 4
- head_weight: bfloat16 [1152, 1152], P('mp'), may hold values from -0.1875 to 0.1875
- text_embeds: bfloat16 [40960, 1152], P('dp', 'mp'), may hold values from -4 to 4
- logit_scale: float32 [1], replicated, may hold values from 72 to 96
- logit_bias: float32 [1], replicated, may hold values from -10 to -5
- labels: int32 [128, 320], P('dp'), may hold values from 0 to 319, each once within a row
- plan: int32 [7], replicated, may hold values from 0 to 6, as said below
Outputs:
- head_grad: float32 [1152, 1152], P('mp')
- text_grad: float32 [40960, 1152], P('dp', 'mp')
Inputs may be any that keep to these rules, and one draw needn't show every extreme that they name: plan[r] is the binary digit in which round r + 1's partner differs from round r's; round 0 pairs each block with itself; the flips follow the reflected binary Gray order over log2(8) distinct digits, which always include digit 0 and digit 6, so the 8 partners are distinct and the last one differs from the block itself in one digit. Each row of labels is a permutation of the rows of one block.
All inputs are finite; a program needn't handle non-finite values.
Results may differ from a plain program's by a relative error of at most 0.0063.
Values may be sent and summed in bfloat16 or wider, within the bound.
No kernel may reach another device: no remote copies, remote signals or barrier semaphores. Data moves between devices by JAX's collectives and lax.ppermute only.
A program may use at most 32 MiB of HBM per device.

v0:
```python
from functools import partial

import jax
import jax.numpy as jnp
from jax import lax
from jax.sharding import PartitionSpec as P

epsilon = 1e-06


def for_sending(shard):

    def short(part):
        return part.astype(jnp.bfloat16) if part.dtype == jnp.float32 else part

    return jax.tree.map(short, shard)


def partner(shard, axis, stride):
    return lax.ppermute(shard, axis, [(i, i ^ 1 << stride) for i in range(lax.axis_size(axis))])


def move_text(block, bit_index):
    return jax.tree.map(
        lambda part, own: part.astype(own.dtype),
        partner(for_sending(block), "dp", bit_index),
        block,
    )


def move_grads(block, bit_index):
    return partner(block, "dp", bit_index)


def signed_grad(score, label_hit, is_first, scale_value, bias_value):
    logits = scale_value * score + bias_value
    positive = jnp.logical_and(is_first, label_hit)
    label_sign = jnp.where(positive, 1.0, -1.0).astype(jnp.float32)
    return (-label_sign * jax.nn.sigmoid(-label_sign * logits)).astype(jnp.bfloat16)


def on_device(image_feats, head_weight, text_embeds, logit_scale, logit_bias, labels, plan):
    block_rows = image_feats.shape[0]
    share_rows = block_rows // lax.axis_size("mp")
    bit_count = lax.axis_size("dp").bit_length() - 1
    round_total = plan.shape[0] + 1
    embedding = lax.dot_general(
        image_feats, head_weight, (((1,), (1,)), ((), ())), preferred_element_type=jnp.float32
    )
    text_wide = text_embeds.astype(jnp.float32)
    img_square, txt_square = lax.psum(
        (jnp.sum(embedding * embedding, axis=-1), jnp.sum(text_wide * text_wide, axis=-1)), "mp"
    )
    img_rinv = lax.rsqrt(img_square + epsilon)[:, None]
    txt_rinv = lax.rsqrt(txt_square + epsilon)[:, None]
    img_unit = embedding * img_rinv
    img_low = img_unit.astype(jnp.bfloat16)
    txt_unit = text_wide * txt_rinv
    txt_low = txt_unit.astype(jnp.bfloat16)
    scale_value = logit_scale[0]
    bias_value = logit_bias[0]
    row_start = lax.axis_index("mp") * share_rows
    block_labels = labels[0]
    local_labels = lax.dynamic_slice_in_dim(block_labels, row_start, share_rows)
    columns = lax.broadcasted_iota(jnp.int32, (share_rows, block_rows), 1)
    label_hit = columns == local_labels[:, None]

    def tile_for(visitor, is_first):
        score = lax.psum_scatter(
            lax.dot_general(
                img_low, visitor, (((1,), (1,)), ((), ())), preferred_element_type=jnp.float32
            ),
            "mp",
            scatter_dimension=0,
            tiled=True,
        )
        prob_share = signed_grad(score, label_hit, is_first, scale_value, bias_value)
        return lax.all_gather(prob_share, "mp", axis=0, tiled=True)

    def accumulate(tile_grad, visitor, img_acc, txt_acc):
        img_acc = img_acc + jnp.dot(tile_grad, visitor, preferred_element_type=jnp.float32)
        txt_acc = txt_acc + lax.dot_general(
            tile_grad, img_low, (((0,), (0,)), ((), ())), preferred_element_type=jnp.float32
        )
        return (img_acc, txt_acc)

    img_zero = jnp.zeros((block_rows, txt_low.shape[1]), jnp.float32)
    txt_zero = jnp.zeros(txt_low.shape, jnp.float32)
    first_tile = tile_for(txt_low, True)
    img_acc, txt_acc = accumulate(first_tile, txt_low, img_zero, txt_zero)
    text_moves = [partial(move_text, bit_index=position) for position in range(bit_count)]
    grad_moves = [partial(move_grads, bit_index=position) for position in range(bit_count)]

    def one_round(round_index, state):
        visitor, img_acc, txt_acc = state
        flip_bit = plan[round_index - 1]
        visitor = lax.switch(flip_bit, text_moves, visitor)
        txt_acc = lax.switch(flip_bit, grad_moves, txt_acc)
        tile_grad = tile_for(visitor, False)
        img_acc, txt_acc = accumulate(tile_grad, visitor, img_acc, txt_acc)
        return (visitor, img_acc, txt_acc)

    visitor, img_acc, txt_acc = lax.fori_loop(
        1, round_total, one_round, (txt_low, img_acc, txt_acc)
    )
    img_dir = scale_value * img_acc
    image_part = jnp.sum(img_unit * img_dir, axis=-1)
    image_dot = lax.psum(image_part, "mp")
    parity = (
        jnp.sum(
            (plan[:, None] == jnp.arange(bit_count, dtype=jnp.int32)[None, :]).astype(jnp.int32),
            axis=0,
        )
        % 2
    )
    for position in range(bit_count):
        moved_back = partner(txt_acc, "dp", position)
        txt_acc = jnp.where(parity[position] == 1, moved_back, txt_acc)
    txt_dir = scale_value * txt_acc
    text_part = jnp.sum(txt_unit * txt_dir, axis=-1)
    text_dot = lax.psum(text_part, "mp")
    img_grad = (img_rinv * (img_dir - img_unit * image_dot[:, None])).astype(jnp.bfloat16)
    head_part = lax.dot_general(
        img_grad, image_feats, (((0,), (0,)), ((), ())), preferred_element_type=jnp.float32
    )
    head_grad = lax.psum(head_part, "dp")
    text_grad = txt_rinv * (txt_dir - txt_unit * text_dot[:, None])
    return (head_grad, text_grad)


def solution(mesh):
    return jax.shard_map(
        on_device,
        mesh=mesh,
        in_specs=(P("dp", None), P("mp", None), P("dp", "mp"), P(), P(), P("dp", None), P()),
        out_specs=(P("mp", None), P("dp", "mp")),
        check_vma=False,
    )
```

profile of v0, /device:TPU:1, one launch (start us, length us, event | category | flops | bytes accessed | tf_op | source)
XLA Modules:
  0.0 2290.4 jit_solution(4467839057114657034)
XLA Ops:
  9.8 16.9 all-reduce.3
  30.2 49.7 %reduce-scatter.6.cloned.1.call-done = f32[40,320]{1,0:T(8,128)} async-done(((f32[320,320]{1,0:T(8,128)}), f32[40,320]{1,0:T(8,128)}) %reduce-scatter.6.cloned.1.call-update) | async-done | bytes 51216
  80.9 22.8 all_gather.16
  104.2 1008.1 %while.63 = (s32[]{:T(128)}, bf16[320,144]{1,0:T(8,128)(2,1)S(1)}, f32[320,144]{0,1:T(8,128)S(1)}, f32[320,144]{0,1:T(8,128)S(1)}, s32[7]{0:T(128)S(1)}, /*index...) while((s32[]{:T(128)}, bf16[320,144]{1,0:T(8,128)(2,1)S(1)}, ...), condition=%wide.region_21.22_spmd, body=%wide.region_5.21_spmd.sunk | while | flops 88744960 | bytes 7086437 | solution.py:103
  105.5 14.6 conditional.4
  105.5 13.4 collective-permute-start
  128.7 83.5 %all-reduce.11.cloned.1.call-done = f32[320,320]{0,1:T(8,128)} async-done(((f32[320,320]{0,1:T(8,128)}), f32[320,320]{0,1:T(8,128)}) %all-reduce.11.cloned.1.call-update) | async-done | bytes 409616 | tf_op jit(solution)/shard_map/while
  214.8 22.3 all_gather.18
  239.9 16.4 conditional.4
  240.0 8.4 collective-permute-start.3
  248.3 8.1 collective-permute-done.3
  259.3 22.8 conditional.5
  261.8 20.2 collective-permute-done.10
  284.1 88.7 %all-reduce.11.cloned.1.call-done = f32[320,320]{0,1:T(8,128)} async-done(((f32[320,320]{0,1:T(8,128)}), f32[320,320]{0,1:T(8,128)}) %all-reduce.11.cloned.1.call-update) | async-done | bytes 409616 | tf_op jit(solution)/shard_map/while
  375.3 22.3 all_gather.18
  400.4 15.0 conditional.4
  400.4 13.8 collective-permute-start
  424.1 84.1 %all-reduce.11.cloned.1.call-done = f32[320,320]{0,1:T(8,128)} async-done(((f32[320,320]{0,1:T(8,128)}), f32[320,320]{0,1:T(8,128)}) %all-reduce.11.cloned.1.call-update) | async-done | bytes 409616 | tf_op jit(solution)/shard_map/while
  510.7 22.3 all_gather.18
  535.8 10.2 conditional.4
  549.0 14.9 conditional.5
  556.1 7.6 collective-permute-done.13
  565.8 88.8 %all-reduce.11.cloned.1.call-done = f32[320,320]{0,1:T(8,128)} async-done(((f32[320,320]{0,1:T(8,128)}), f32[320,320]{0,1:T(8,128)}) %all-reduce.11.cloned.1.call-update) | async-done | bytes 409616 | tf_op jit(solution)/shard_map/while
  657.1 22.3 all_gather.18
  682.2 15.0 conditional.4
  682.2 13.8 collective-permute-start
  705.9 84.1 %all-reduce.11.cloned.1.call-done = f32[320,320]{0,1:T(8,128)} async-done(((f32[320,320]{0,1:T(8,128)}), f32[320,320]{0,1:T(8,128)}) %all-reduce.11.cloned.1.call-update) | async-done | bytes 409616 | tf_op jit(solution)/shard_map/while
  792.5 22.3 all_gather.18
  817.7 16.4 conditional.4
  817.7 8.4 collective-permute-start.3
  826.0 8.1 collective-permute-done.3
  837.0 22.8 conditional.5
  839.5 20.2 collective-permute-done.10
  861.8 88.7 %all-reduce.11.cloned.1.call-done = f32[320,320]{0,1:T(8,128)} async-done(((f32[320,320]{0,1:T(8,128)}), f32[320,320]{0,1:T(8,128)}) %all-reduce.11.cloned.1.call-update) | async-done | bytes 409616 | tf_op jit(solution)/shard_map/while
  953.0 22.3 all_gather.18
  978.1 15.0 conditional.4
  978.2 13.8 collective-permute-start
  1001.8 84.1 %all-reduce.11.cloned.1.call-done = f32[320,320]{0,1:T(8,128)} async-done(((f32[320,320]{0,1:T(8,128)}), f32[320,320]{0,1:T(8,128)}) %all-reduce.11.cloned.1.call-update) | async-done | bytes 409616 | tf_op jit(solution)/shard_map/while
  1088.5 22.3 all_gather.18
  1112.4 13.8 collective-permute-start.14
  1141.6 8.9 collective-permute-done.16
  1150.6 7.6 collective-permute-start.17
  1158.8 18.5 collective-permute-done.17
  1177.4 11.8 collective-permute-start.18
  1189.8 19.0 collective-permute-done.18
  1213.6 8.6 collective-permute-done.19
  1237.6 13.2 all-reduce.2
  1252.8 1029.1 %all-reduce.9.cloned.1.call-done = f32[144,1152]{1,0:T(8,128)} async-done(((f32[144,1152]{1,0:T(8,128)}), f32[144,1152]{1,0:T(8,128)}) %all-reduce.9.cloned.1.call-update) | async-done | bytes 663568 | tf_op jit(solution)/shard_map/psum | solution.py:126
  (155 shorter events, 162.3 us)
Async XLA Ops:
  7.2 1.2 copy-start
  7.2 72.8 %reduce-scatter.6.cloned.1.call-start = ((), (), s32[]{:S(2)}) async-start(), calls=%async_computation.2 | async-start | bytes 552960
  8.3 18.3 copy-start.1
  29.4 0.8 copy-start.2
  104.2 108.1 %all-reduce.11.cloned.1.call-start = ((), (), s32[]{:S(2)}) async-start(), calls=%async_computation.3 | async-start | bytes 983040 | tf_op jit(solution)/shard_map/while
  105.5 14.5 collective-permute-start
  123.1 3.5 collective-permute-start.7
  238.6 134.1 %all-reduce.11.cloned.1.call-start = ((), (), s32[]{:S(2)}) async-start(), calls=%async_computation.3 | async-start | bytes 983040 | tf_op jit(solution)/shard_map/while
  240.0 16.4 collective-permute-start.3
  259.5 22.5 collective-permute-start.10
  399.1 109.1 %all-reduce.11.cloned.1.call-start = ((), (), s32[]{:S(2)}) async-start(), calls=%async_computation.3 | async-start | bytes 983040 | tf_op jit(solution)/shard_map/while
  400.4 15.0 collective-permute-start
  418.5 3.5 collective-permute-start.7
  534.5 120.0 %all-reduce.11.cloned.1.call-start = ((), (), s32[]{:S(2)}) async-start(), calls=%async_computation.3 | async-start | bytes 983040 | tf_op jit(solution)/shard_map/while
  535.9 10.2 collective-permute-start.6
  549.1 14.6 collective-permute-start.13
  680.9 109.1 %all-reduce.11.cloned.1.call-start = ((), (), s32[]{:S(2)}) async-start(), calls=%async_computation.3 | async-start | bytes 983040 | tf_op jit(solution)/shard_map/while
  682.2 15.0 collective-permute-start
  700.3 3.5 collective-permute-start.7
  816.4 134.1 %all-reduce.11.cloned.1.call-start = ((), (), s32[]{:S(2)}) async-start(), calls=%async_computation.3 | async-start | bytes 983040 | tf_op jit(solution)/shard_map/while
  817.7 16.4 collective-permute-start.3
  837.2 22.5 collective-permute-start.10
  976.9 109.1 %all-reduce.11.cloned.1.call-start = ((), (), s32[]{:S(2)}) async-start(), calls=%async_computation.3 | async-start | bytes 983040 | tf_op jit(solution)/shard_map/while
  978.2 15.0 collective-permute-start
  996.2 3.5 collective-permute-start.7
  1112.3 1169.6 %all-reduce.9.cloned.1.call-start = ((), (), s32[]{:S(2)}) async-start(), calls=%async_computation.1 | async-start | bytes 1327104 | tf_op jit(solution)/shard_map/psum | solution.py:126
  1112.4 15.2 collective-permute-start.14
  1127.6 9.0 collective-permute-start.15
  1136.6 14.0 collective-permute-start.16
  1150.6 26.7 %collective-permute-start.17 = (f32[320,144]{0,1:T(8,128)S(1)}, f32[320,144]{0,1:T(8,128)S(1)}, u32[]{:S(2)}, u32[]{:S(2)}) collective-permute-start(f32[320,144]{0,1:T(8,128)S(1)} %broadcast_select_fusion.2), channel_id=1, source_target_pairs={{0,64},{8,72},{16,80},{24,88},{32,96},{40,104},{48,112},{56,120},{... | collective-permute-start | bytes 552968 | tf_op jit(solution)/shard_map/ppermute | solution.py:20
  1177.4 31.5 %collective-permute-start.18 = (f32[320,144]{0,1:T(8,128)S(1)}, f32[320,144]{0,1:T(8,128)S(1)}, u32[]{:S(2)}, u32[]{:S(2)}) collective-permute-start(f32[320,144]{0,1:T(8,128)S(1)} %broadcast_select_fusion.3), channel_id=1, source_target_pairs={{0,128},{8,136},{16,144},{24,152},{32,160},{40,168},{48,176},{56,1... | collective-permute-start | bytes 552968 | tf_op jit(solution)/shard_map/ppermute | solution.py:20
  1208.9 13.3 collective-permute-start.19
  1222.2 15.3 collective-permute-start.20
Sparse Core Ops, SparseCore 0:
  27.9 51.9 reduce-scatter.5
  122.2 90.0 all-reduce.10
  258.5 114.1 all-reduce.10
  417.5 90.6 all-reduce.10
  548.2 106.3 all-reduce.10
  699.3 90.6 all-reduce.10
  836.2 114.2 all-reduce.10
  995.3 90.6 all-reduce.10
  1252.1 1029.7 all-reduce.8
where the time goes:
time: 2280 us; the launch traced here: 2290 us
  waiting for transfers between devices  1830 us (80%)
  blocking collectives  209 us (9%)
  starting transfers between devices  152 us (7%)
  local copies, waits for them, and re-layouts  33.6 us (1%)
  matrix products  28.7 us (1%)
    psum x1, waiting for transfers between devices, on_device(): head_grad = lax.psum(head_part, 'dp')  1030 us
    while x14, waiting for transfers between devices  602 us
    all_gather x8, blocking collectives, tile_for(): return lax.all_gather(prob_share, 'mp', axis=0, tiled=True)  179 us
    ppermute x21, starting transfers between devices, partner(): lax.ppermute(shard, axis, [(i, i ^ 1 << stride) for i in range(lax.axis_s...  152 us
    ppermute x21, waiting for transfers between devices, partner(): lax.ppermute(shard, axis, [(i, i ^ 1 << stride) for i in range(lax.axis_s...  144 us
    unnamed x3, waiting for transfers between devices  49.7 us
  transfers between devices with their start and end apart: 30, of which 29 were waited for; matrix products, arithmetic and copies ran while one was open for 1% of the time, Pallas kernels for 0%

commit v1 on v0

v1 whole, which is shorter than its diff:
```python
import jax
import jax.numpy as jnp
from jax import lax
from jax.experimental import pallas as pl
from jax.experimental.pallas import tpu as pltpu
from jax.sharding import Mesh
from jax.sharding import PartitionSpec as P

EPSILON = 1e-06
LANES = 128
ROW_TILE = 16
SWAP = [(0, 1), (1, 0)]
VMEM_LIMIT = 48 * 1024 * 1024


def swap(shard, axis):
    return lax.ppermute(shard, axis, SWAP)


def swap_both(shard, first, second):
    return lax.ppermute(shard, (first, second), [(i, i ^ 3) for i in range(4)])


def exchange(parts, axes):
    return lax.all_to_all(parts, axes, 0, 0, tiled=False)


def gather(shard, axes, count):
    return exchange(jnp.broadcast_to(shard[None], (count,) + shard.shape), axes)


def tile_kernel(number_ref, first_ref, label_ref, embed_ref, text_ref, out_ref):
    scale = number_ref[0]
    bias = number_ref[1]
    parts, double_width, rows = out_ref.shape
    width = double_width // 2
    embed = embed_ref[...]
    img_rinv = lax.rsqrt(jnp.sum(embed * embed, axis=0, keepdims=True) + EPSILON)
    img_unit = embed * img_rinv
    img_low = img_unit.astype(jnp.bfloat16)
    text = text_ref[...].astype(jnp.float32)
    txt_rinv = lax.rsqrt(jnp.sum(text * text, axis=0, keepdims=True) + EPSILON)
    txt_unit = text * txt_rinv
    txt_low = txt_unit.astype(jnp.bfloat16)
    score = lax.dot_general(
        txt_low, img_low, (((0,), (0,)), ((), ())), preferred_element_type=jnp.float32
    )
    logits = scale * score + bias
    text_ids = lax.broadcasted_iota(jnp.int32, score.shape, 0)
    own_text = jnp.where(first_ref[0] == 0, label_ref[...], -1)
    label_sign = jnp.where(text_ids == own_text, 1.0, -1.0).astype(jnp.float32)
    tile_grad = (-label_sign * jax.nn.sigmoid(-label_sign * logits)).astype(jnp.bfloat16)
    img_dir = scale * jnp.dot(txt_low, tile_grad, preferred_element_type=jnp.float32)
    image_dot = jnp.sum(img_unit * img_dir, axis=0, keepdims=True)
    img_part = (img_rinv * (img_dir - img_unit * image_dot)).astype(out_ref.dtype)
    out_ref[:, :width, :] = img_part.reshape(parts, width, rows)
    txt_dir = scale * lax.dot_general(
        img_low, tile_grad, (((1,), (1,)), ((), ())), preferred_element_type=jnp.float32
    )
    text_dot = jnp.sum(txt_unit * txt_dir, axis=0, keepdims=True)
    txt_part = (txt_rinv * (txt_dir - txt_unit * text_dot)).astype(out_ref.dtype)
    out_ref[:, width:, :] = txt_part.reshape(parts, width, rows)


def tile_parts(numbers, mp_index, labels, embed, text, parts):
    width, rows = embed.shape
    smem = pl.BlockSpec(memory_space=pltpu.SMEM)
    vmem = pl.BlockSpec(memory_space=pltpu.VMEM)
    return pl.pallas_call(
        tile_kernel,
        out_shape=jax.ShapeDtypeStruct((parts, 2 * width // parts, rows), jnp.bfloat16),
        in_specs=[smem, smem, vmem, vmem, vmem],
        out_specs=vmem,
        compiler_params=pltpu.CompilerParams(vmem_limit_bytes=VMEM_LIMIT),
        name="tile_parts",
    )(numbers, mp_index, labels, embed, text)


def head_kernel(part_ref, feats_ref, out_ref):
    columns = part_ref.shape[1]
    img_grad = jnp.sum(part_ref[...].astype(jnp.float32), axis=0).astype(jnp.bfloat16)
    used = 0
    for start in range(0, feats_ref.shape[1], LANES):
        product = jnp.dot(
            img_grad, feats_ref[:, start : start + LANES], preferred_element_type=jnp.float32
        )
        out_ref[used : used + columns, :] = product.astype(out_ref.dtype)
        used += columns
    if used < out_ref.shape[0]:
        out_ref[used:, :] = jnp.zeros((out_ref.shape[0] - used, LANES), out_ref.dtype)


def head_rows(img_parts, feats, total_rows):
    vmem = pl.BlockSpec(memory_space=pltpu.VMEM)
    return pl.pallas_call(
        head_kernel,
        out_shape=jax.ShapeDtypeStruct((total_rows, LANES), jnp.bfloat16),
        in_specs=[vmem, vmem],
        out_specs=vmem,
        compiler_params=pltpu.CompilerParams(vmem_limit_bytes=VMEM_LIMIT),
        name="head_rows",
    )(img_parts, feats)


def summed(parts):
    return jnp.sum(parts.astype(jnp.float32), axis=0)


def round_up(value, step):
    return -(-value // step) * step


def solution(mesh):
    dp, mp = mesh.shape["dp"], mesh.shape["mp"]
    bits = dp.bit_length() - 1
    names = tuple(f"b{bit}" for bit in reversed(range(bits)))
    fine = Mesh(mesh.devices.reshape((2,) * bits + (mp,)), names + ("mp",))
    core, top = "b0", names[0]
    far, near = names[:2], names[2:-1]
    near_count, far_count = 2 ** len(near), 2 ** len(far)

    def reduce_head(rows):
        rows = rows.reshape(2, near_count, -1, LANES)
        rows = summed(exchange(rows, core)).astype(jnp.bfloat16)
        rows = summed(exchange(rows, near))
        rows = summed(gather(rows, far, far_count)).astype(jnp.bfloat16)
        rows = gather(rows, near, near_count)
        return gather(rows, core, 2).reshape(-1, LANES)

    def with_middle(middle, feats, weight, text, scale, bias, labels):
        share, width = weight.shape
        rows = feats.shape[0]
        own = text.T
        by_middle = swap(own, middle)
        by_top = swap(own, top)
        by_both = swap_both(own, top, middle)
        embedding = lax.dot_general(
            weight, feats, (((1,), (1,)), ((), ())), preferred_element_type=jnp.float32
        )
        embedding = gather(embedding, "mp", mp).reshape(width, rows)
        four = jnp.stack([own, by_middle, by_top, by_both])
        eight = jnp.concatenate([four, swap(four, core)])
        met_text = exchange(eight, "mp").reshape(width, rows)
        numbers = jnp.concatenate([scale, bias])
        mp_index = lax.axis_index("mp").astype(jnp.int32).reshape(1)
        parts = tile_parts(numbers, mp_index, labels, embedding, met_text, mp)
        parts = exchange(parts, "mp")
        total_rows = round_up(share * width // LANES, 2 * near_count * ROW_TILE)
        head = head_rows(parts[:, :share], feats, total_rows)
        text_parts = parts[:, share:]
        half = mp // 2
        back = swap(text_parts[half:], core)
        text_four = text_parts[:half].astype(jnp.float32) + back.astype(jnp.float32)
        back = swap(text_four[2:].astype(jnp.bfloat16), top)
        text_two = text_four[:2] + back.astype(jnp.float32)
        back = swap(text_two[1].astype(jnp.bfloat16), middle)
        text_grad = (text_two[0] + back.astype(jnp.float32)).T
        head = reduce_head(head)[: share * width // LANES]
        head = head.reshape(width // LANES, share, LANES).transpose(1, 0, 2).reshape(share, width)
        return head.astype(jnp.float32), text_grad

    def on_device(feats, weight, text, scale, bias, labels, plan):
        middle_bit = jnp.max(jnp.where(plan == bits - 1, 0, plan))
        branches = [
            (lambda *args, name=f"b{bit}": with_middle(name, *args)) for bit in range(1, bits - 1)
        ]
        return lax.switch(middle_bit - 1, branches, feats, weight, text, scale, bias, labels)

    return jax.shard_map(
        on_device,
        mesh=fine,
        in_specs=(P(names, None), P("mp", None), P(names, "mp"), P(), P(), P(names, None), P()),
        out_specs=(P("mp", None), P(names, "mp")),
        check_vma=False,
    )
```

time: 2280 us -> 201 us (0.09)
  waiting for transfers between devices: 1830 us -> 59.1 us
  blocking collectives: 209 us -> 56.1 us
  starting transfers between devices: 152 us -> 66.3 us
  matrix products: 28.7 us -> 0.41 us
  local copies, waits for them, and re-layouts: 33.6 us -> 7.57 us
    psum x1 -> x0, waiting for transfers between devices: 1030 us -> none  [on_device(): head_grad = lax.psum(head_part, 'dp')]
    while x14 -> x0, waiting for transfers between devices: 602 us -> none
    all_gather x8 -> x0, blocking collectives: 179 us -> none  [tile_for(): return lax.all_gather(prob_share, 'mp', axis=0, tiled=True)]
    ppermute x21 -> x7, waiting for transfers between devices: 144 us -> 16 us  [the longest x1 8.89 us: swap_both(): return lax.ppermute(shard, (first, second), [(i, i ^ 3) for i in range(4)])]
    ppermute x21 -> x7, starting transfers between devices: 152 us -> 32.6 us  [the longest x6 30.7 us: swap(): return lax.ppermute(shard, axis, SWAP)]
    all_to_all x0 -> x4, blocking collectives: none -> 56.1 us  [exchange(): return lax.all_to_all(parts, axes, 0, 0, tiled=False)]
    unnamed x3 -> x0, waiting for transfers between devices: 49.7 us -> none
    all_to_all x0 -> x4, waiting for transfers between devices: none -> 43.1 us  [exchange(): return lax.all_to_all(parts, axes, 0, 0, tiled=False)]
  transfers between devices with their start and end apart: 30 -> 11, of which waited for: 29 -> 7; matrix products, arithmetic and copies ran while one was open for 1% -> 3% of each run, Pallas kernels for 0% -> 0%
where the time goes in v1:
time: 201 us; the launch traced here: 200 us
  starting transfers between devices  66.3 us (33%)
  waiting for transfers between devices  59.1 us (29%)
  blocking collectives  56.1 us (28%)
  local copies, waits for them, and re-layouts  7.57 us (4%)
  other arithmetic  4.7 us (2%)
  Pallas kernels  4.17 us (2%)
    all_to_all x4, blocking collectives, exchange(): return lax.all_to_all(parts, axes, 0, 0, tiled=False)  56.1 us
    all_to_all x4, waiting for transfers between devices, exchange(): return lax.all_to_all(parts, axes, 0, 0, tiled=False)  43.1 us
    all_to_all x4, starting transfers between devices, exchange(): return lax.all_to_all(parts, axes, 0, 0, tiled=False)  33.7 us
    ppermute x6, starting transfers between devices, swap(): return lax.ppermute(shard, axis, SWAP)  30.7 us
    ppermute x1, waiting for transfers between devices, swap_both(): return lax.ppermute(shard, (first, second), [(i, i ^ 3) for i in range(4)])  8.89 us
    ppermute x6, waiting for transfers between devices, swap(): return lax.ppermute(shard, axis, SWAP)  7.1 us
    unnamed x14, local copies, waits for them, and re-layouts  4.43 us
  transfers between devices with their start and end apart: 11, of which 7 were waited for; matrix products, arithmetic and copies ran while one was open for 3% of the time, Pallas kernels for 0%

profile of v1, /device:TPU:1, one launch (start us, length us, event | category | flops | bytes accessed | tf_op | source)
XLA Modules:
  0.0 200.4 jit_solution(1135938686650152979)
XLA Ops:
  0.6 1.3 fusion.15
  2.6 196.9 %conditional.4 = (f32[320,144]{0,1:T(8,128)S(1)}, f32[144,1152]{1,0:T(8,128)S(1)}) conditional(s32[]{:T(128)} %clamp.3, (f32[1]{0:T(128)}, f32[1]{0:T(128)}, bf16[144,1152]{1,0:T(8,128)(2,1)}, bf16[320,1152]{1,0:T(8,128)(2,1)}, bf16[320,144]{0,1:T(8,128)(2,1)}, /*index=5*/s32[1,320]{1,0:T(1,128)}) %tuple.50, ...), branch_computations={%region_1.5_spmd, %region_5.9_spmd, %region_9.13_spmd, %region_13.... | conditional | flops 108023808 | bytes 37256744
  2.6 6.6 %collective-permute-start.7 = (bf16[144,320]{1,0:T(8,128)(2,1)}, bf16[144,320]{1,0:T(8,128)(2,1)S(1)}, u32[]{:S(2)}, u32[]{:S(2)}) collective-permute-start(bf16[144,320]{1,0:T(8,128)(2,1)} %bitcast.184), channel_id=1, source_target_pairs={{0,32},{32,0},{1,33},{33,1},{2,34},{34,2},{3,35},{35,3},{4,36},{36... | collective-permute-start | bytes 276488 | tf_op jit(solution)/shard_map/cond/branch_1_fun/ppermute | solution.py:17
  9.2 7.5 %collective-permute-start.8 = (bf16[144,320]{1,0:T(8,128)(2,1)}, bf16[144,320]{1,0:T(8,128)(2,1)S(1)}, u32[]{:S(2)}, u32[]{:S(2)}) collective-permute-start(bf16[144,320]{1,0:T(8,128)(2,1)} %bitcast.185), channel_id=1, source_target_pairs={{0,512},{512,0},{1,513},{513,1},{2,514},{514,2},{3,515},{515,3},{4... | collective-permute-start | bytes 276488 | tf_op jit(solution)/shard_map/cond/branch_1_fun/ppermute | solution.py:17
  16.7 1.9 collective-permute-start.9
  18.6 1.6 constant_dynamic-update-slice_fusion.9
  20.2 0.0 collective-permute-done.8
  20.2 8.9 %collective-permute-done.9 = bf16[144,320]{1,0:T(8,128)(2,1)S(1)} collective-permute-done((bf16[144,320]{1,0:T(8,128)(2,1)}, bf16[144,320]{1,0:T(8,128)(2,1)S(1)}, u32[]{:S(2)}, u32[]{:S(2)}) %collective-permute-start.9) | collective-permute-done | bytes 92192 | tf_op jit(solution)/shard_map/cond/branch_1_fun/ppermute | solution.py:21
  29.1 1.0 pad_maximum_fusion.2
  30.1 0.0 copy-start.1
  30.1 0.0 copy-start.6
  30.1 6.9 %collective-permute-start.10 = (bf16[4,144,320]{2,1,0:T(8,128)(2,1)S(1)}, bf16[4,144,320]{2,1,0:T(8,128)(2,1)S(1)}, u32[]{:S(2)}, u32[]{:S(2)}) collective-permute-start(bf16[4,144,320]{2,1,0:T(8,128)(2,1)S(1)} %pad_maximum_fusion.2), channel_id=1, source_target_pairs={{0,8},{8,0},{1,9},{9,1},{2,10},{10,2},{3,11},{11,3},{4,12},{12,4},... | collective-permute-start | bytes 1105928 | tf_op jit(solution)/shard_map/cond/branch_1_fun/ppermute | solution.py:17
  37.0 0.7 constant_dynamic-update-slice_fusion.8
  37.7 0.7 constant_dynamic-update-slice_fusion.7
  38.4 0.6 constant_dynamic-update-slice_fusion.6
  39.0 0.8 constant_dynamic-update-slice_fusion.5
  39.8 3.5 %all-to-all-start.9 = ((bf16[8,144,320]{2,1,0:T(8,128)(2,1)}), bf16[8,144,320]{2,1,0:T(8,128)(2,1)S(1)}, u32[]{:S(2)}, u32[]{:S(2)}) async-start(bf16[8,144,320]{2,1,0:T(8,128)(2,1)} %constant_dynamic-update-slice_fusion.5), calls=%async_computation.9 | async-start | bytes 1769472 | tf_op jit(solution)/shard_map/cond/branch_1_fun/all_to_all | solution.py:25
  43.4 0.4 fusion.17
  43.8 13.6 %all-to-all-done.9 = bf16[8,144,320]{2,1,0:T(8,128)(2,1)S(1)} async-done(((bf16[8,144,320]{2,1,0:T(8,128)(2,1)}), bf16[8,144,320]{2,1,0:T(8,128)(2,1)S(1)}, u32[]{:S(2)}, u32[]{:S(2)}) %all-to-all-start.9) | async-done | bytes 737312 | tf_op jit(solution)/shard_map/cond/branch_1_fun/all_to_all | solution.py:25
  57.5 1.3 broadcast_in_dim.43
  58.8 3.7 %all-to-all-start.8 = ((f32[8,144,320]{2,1,0:T(8,128)}), f32[8,144,320]{2,1,0:T(8,128)S(1)}, u32[]{:S(2)}, u32[]{:S(2)}) async-start(f32[8,144,320]{2,1,0:T(8,128)} %broadcast_in_dim.43), calls=%async_computation.8 | async-start | bytes 3538944 | tf_op jit(solution)/shard_map/cond/branch_1_fun/all_to_all | solution.py:25
  62.6 1.4 pad_maximum_fusion.3.number_ref
  63.9 21.3 %all-to-all-done.8 = f32[8,144,320]{2,1,0:T(8,128)S(1)} async-done(((f32[8,144,320]{2,1,0:T(8,128)}), f32[8,144,320]{2,1,0:T(8,128)S(1)}, u32[]{:S(2)}, u32[]{:S(2)}) %all-to-all-start.8) | async-done | bytes 1474592 | tf_op jit(solution)/shard_map/cond/branch_1_fun/all_to_all | solution.py:25
  85.2 3.6 %tile_parts.6 = bf16[8,288,320]{2,1,0:T(8,128)(2,1)S(1)} custom-call(f32[2]{0:T(128)S(1)} %pad_maximum_fusion.3.number_ref, s32[1]{0:T(128)} %bitcast.16.first_ref, s32[1,320]{1,0:T(1,128)S(1)} %copy-done.13, f32[1152,320]{1,0:T(8,128)S(1)} %bitcast.166, bf16[1152,320]{1,0:T(8,128)(2,1)S(1)} %bitcast.171), custom_call_target="tpu_custom_call" | custom-call | tf_op jit(solution)/shard_map/cond/branch_1_fun/tile_parts/pallas_call | solution.py:69
  88.9 26.3 %all_to_all.164 = bf16[8,288,320]{2,1,0:T(8,128)(2,1)S(1)} all-to-all(bf16[8,288,320]{2,1,0:T(8,128)(2,1)S(1)} %tile_parts.6), channel_id=1, replica_groups=mesh['b6'=2,'b5'=2,'b4'=2,'b3'=2,'b2'=2,'b1'=2,'b0'=2,'mp'=8] {'mp'}, dimensions={0} | all-to-all | bytes 2949120 | tf_op jit(solution)/shard_map/cond/branch_1_fun/all_to_all | solution.py:25
  115.1 0.1 slice.159.part_ref
  115.2 0.6 head_rows.6
  115.8 5.4 %all_to_all.165 = bf16[2,16,48,128]{3,2,1,0:T(8,128)(2,1)S(1)} all-to-all(bf16[2,16,48,128]{3,2,1,0:T(8,128)(2,1)S(1)} %bitcast.176), channel_id=1, replica_groups=mesh['b6'=2,'b5'=2,'b4'=2,'b3'=2,'b2'=2,'b1'=2,'b0'=2,'mp'=8] {'b0'}, dimensions={0} | all-to-all | bytes 786432 | tf_op jit(solution)/shard_map/cond/branch_1_fun/all_to_all | solution.py:25
  121.2 0.8 reduce_sum.138
  122.0 15.7 %all-to-all-start.12 = ((bf16[16,48,128]{2,1,0:T(8,128)(2,1)}), bf16[16,48,128]{2,1,0:T(8,128)(2,1)S(1)}, u32[]{:S(2)}, u32[]{:S(2)}) async-start(bf16[16,48,128]{2,1,0:T(8,128)(2,1)} %reduce_sum.138), calls=%async_computation.12 | async-start | bytes 393216 | tf_op jit(solution)/shard_map/cond/branch_1_fun/all_to_all | solution.py:25
  137.8 2.6 %collective-permute-start.11 = (bf16[4,144,320]{2,1,0:T(8,128)(2,1)S(1)}, bf16[4,144,320]{2,1,0:T(8,128)(2,1)S(1)}, u32[]{:S(2)}, u32[]{:S(2)}) collective-permute-start(bf16[4,144,320]{2,1,0:T(8,128)(2,1)S(1)} %slice.154), channel_id=1, source_target_pairs={{0,8},{8,0},{1,9},{9,1},{2,10},{10,2},{3,11},{11,3},{4,12},{12,4},... | collective-permute-start | bytes 1105928 | tf_op jit(solution)/shard_map/cond/branch_1_fun/ppermute | solution.py:17
  140.4 1.4 collective-permute-done.11
  141.8 0.1 convert_add_fusion.1
  141.9 3.0 %collective-permute-start.12 = (bf16[2,144,320]{2,1,0:T(8,128)(2,1)S(1)}, bf16[2,144,320]{2,1,0:T(8,128)(2,1)S(1)}, u32[]{:S(2)}, u32[]{:S(2)}) collective-permute-start(bf16[2,144,320]{2,1,0:T(8,128)(2,1)S(1)} %slice.241), channel_id=1, source_target_pairs={{0,512},{512,0},{1,513},{513,1},{2,514},{514,2},{3,515},{515,3},{4... | collective-permute-start | bytes 552968 | tf_op jit(solution)/shard_map/cond/branch_1_fun/ppermute | solution.py:17
  144.8 5.8 %all-to-all-done.12 = bf16[16,48,128]{2,1,0:T(8,128)(2,1)S(1)} async-done(((bf16[16,48,128]{2,1,0:T(8,128)(2,1)}), bf16[16,48,128]{2,1,0:T(8,128)(2,1)S(1)}, u32[]{:S(2)}, u32[]{:S(2)}) %all-to-all-start.12) | async-done | bytes 196640 | tf_op jit(solution)/shard_map/cond/branch_1_fun/all_to_all | solution.py:25
  150.7 10.4 %all_to_all.166 = f32[4,48,128]{2,1,0:T(8,128)S(1)} all-to-all(f32[4,48,128]{2,1,0:T(8,128)S(1)} %broadcast_in_dim.44), channel_id=1, replica_groups=mesh['b6'=2,'b5'=2,'b4'=2,'b3'=2,'b2'=2,'b1'=2,'b0'=2,'mp'=8] {'b6','b5'}, dimensions={0} | all-to-all | bytes 196608 | tf_op jit(solution)/shard_map/cond/branch_1_fun/all_to_all | solution.py:25
  161.1 0.7 broadcast_in_dim.45
  161.8 10.7 %all-to-all-start.14 = ((bf16[16,48,128]{2,1,0:T(8,128)(2,1)}), bf16[16,48,128]{2,1,0:T(8,128)(2,1)S(1)}, u32[]{:S(2)}, u32[]{:S(2)}) async-start(bf16[16,48,128]{2,1,0:T(8,128)(2,1)} %broadcast_in_dim.45), calls=%async_computation.14 | async-start | bytes 393216 | tf_op jit(solution)/shard_map/cond/branch_1_fun/all_to_all | solution.py:25
  172.5 0.1 slice_add_fusion.1
  172.5 4.2 %collective-permute-start.13 = (bf16[144,320]{1,0:T(8,128)(2,1)S(1)}, bf16[144,320]{1,0:T(8,128)(2,1)S(1)}, u32[]{:S(2)}, u32[]{:S(2)}) collective-permute-start(bf16[144,320]{1,0:T(8,128)(2,1)S(1)} %fusion.5), channel_id=1, source_target_pairs={{0,32},{32,0},{1,33},{33,1},{2,34},{34,2},{3,35},{35,3},{4,36},{36... | collective-permute-start | bytes 276488 | tf_op jit(solution)/shard_map/cond/branch_1_fun/ppermute | solution.py:17
  176.7 5.7 %collective-permute-done.13 = bf16[144,320]{1,0:T(8,128)(2,1)S(1)} collective-permute-done((bf16[144,320]{1,0:T(8,128)(2,1)S(1)}, bf16[144,320]{1,0:T(8,128)(2,1)S(1)}, u32[]{:S(2)}, u32[]{:S(2)}) %collective-permute-start.13) | collective-permute-done | bytes 92192 | tf_op jit(solution)/shard_map/cond/branch_1_fun/ppermute | solution.py:17
  182.4 2.4 %all-to-all-done.14 = bf16[16,48,128]{2,1,0:T(8,128)(2,1)S(1)} async-done(((bf16[16,48,128]{2,1,0:T(8,128)(2,1)}), bf16[16,48,128]{2,1,0:T(8,128)(2,1)S(1)}, u32[]{:S(2)}, u32[]{:S(2)}) %all-to-all-start.14) | async-done | bytes 196640 | tf_op jit(solution)/shard_map/cond/branch_1_fun/all_to_all | solution.py:25
  184.8 0.1 broadcast_in_dim.46
  184.9 14.0 %all_to_all.167 = bf16[2,16,48,128]{3,2,1,0:T(8,128)(2,1)S(1)} all-to-all(bf16[2,16,48,128]{3,2,1,0:T(8,128)(2,1)S(1)} %broadcast_in_dim.46), channel_id=1, replica_groups=mesh['b6'=2,'b5'=2,'b4'=2,'b3'=2,'b2'=2,'b1'=2,'b0'=2,'mp'=8] {'b0'}, dimensions={0} | all-to-all | bytes 786432 | tf_op jit(solution)/shard_map/cond/branch_1_fun/all_to_all | solution.py:25
  199.5 0.0 copy-start.10
  199.5 0.0 copy-start.11
  199.5 0.8 copy-done.10
  200.3 0.1 copy-done.11
  (16 shorter events, 0.3 us)
Async XLA Ops:
  2.6 17.6 %collective-permute-start.7 = (bf16[144,320]{1,0:T(8,128)(2,1)}, bf16[144,320]{1,0:T(8,128)(2,1)S(1)}, u32[]{:S(2)}, u32[]{:S(2)}) collective-permute-start(bf16[144,320]{1,0:T(8,128)(2,1)} %bitcast.184), channel_id=1, source_target_pairs={{0,32},{32,0},{1,33},{33,1},{2,34},{34,2},{3,35},{35,3},{4,36},{36... | collective-permute-start | bytes 276488 | tf_op jit(solution)/shard_map/cond/branch_1_fun/ppermute | solution.py:17
  9.2 11.0 %collective-permute-start.8 = (bf16[144,320]{1,0:T(8,128)(2,1)}, bf16[144,320]{1,0:T(8,128)(2,1)S(1)}, u32[]{:S(2)}, u32[]{:S(2)}) collective-permute-start(bf16[144,320]{1,0:T(8,128)(2,1)} %bitcast.185), channel_id=1, source_target_pairs={{0,512},{512,0},{1,513},{513,1},{2,514},{514,2},{3,515},{515,3},{4... | collective-permute-start | bytes 276488 | tf_op jit(solution)/shard_map/cond/branch_1_fun/ppermute | solution.py:17
  16.7 12.4 %collective-permute-start.9 = (bf16[144,320]{1,0:T(8,128)(2,1)}, bf16[144,320]{1,0:T(8,128)(2,1)S(1)}, u32[]{:S(2)}, u32[]{:S(2)}) collective-permute-start(bf16[144,320]{1,0:T(8,128)(2,1)} %bitcast.186), channel_id=1, source_target_pairs={{0,544},{32,512},{512,32},{544,0},{1,545},{33,513},{513,33},{545,1... | collective-permute-start | bytes 276488 | tf_op jit(solution)/shard_map/cond/branch_1_fun/ppermute | solution.py:21
  30.1 13.3 %copy-start.1 = (bf16[320,1152]{1,0:T(8,128)(2,1)S(1)}, bf16[320,1152]{1,0:T(8,128)(2,1)}, u32[]{:S(2)}) copy-start(bf16[320,1152]{1,0:T(8,128)(2,1)} %get-tuple-element.78.feats_ref) | copy-start | bytes 2211844
  30.1 13.3 %copy-start.6 = (bf16[144,1152]{1,0:T(8,128)(2,1)S(1)}, bf16[144,1152]{1,0:T(8,128)(2,1)}, u32[]{:S(2)}) copy-start(bf16[144,1152]{1,0:T(8,128)(2,1)} %get-tuple-element.77) | copy-start | bytes 995332
  30.1 8.9 %collective-permute-start.10 = (bf16[4,144,320]{2,1,0:T(8,128)(2,1)S(1)}, bf16[4,144,320]{2,1,0:T(8,128)(2,1)S(1)}, u32[]{:S(2)}, u32[]{:S(2)}) collective-permute-start(bf16[4,144,320]{2,1,0:T(8,128)(2,1)S(1)} %pad_maximum_fusion.2), channel_id=1, source_target_pairs={{0,8},{8,0},{1,9},{9,1},{2,10},{10,2},{3,11},{11,3},{4,12},{12,4},... | collective-permute-start | bytes 1105928 | tf_op jit(solution)/shard_map/cond/branch_1_fun/ppermute | solution.py:17
  39.8 17.6 %all-to-all-start.9 = ((bf16[8,144,320]{2,1,0:T(8,128)(2,1)}), bf16[8,144,320]{2,1,0:T(8,128)(2,1)S(1)}, u32[]{:S(2)}, u32[]{:S(2)}) async-start(bf16[8,144,320]{2,1,0:T(8,128)(2,1)} %constant_dynamic-update-slice_fusion.5), calls=%async_computation.9 | async-start | bytes 1769472 | tf_op jit(solution)/shard_map/cond/branch_1_fun/all_to_all | solution.py:25
  58.8 26.4 %copy-start.13 = (s32[1,320]{1,0:T(1,128)S(1)}, s32[1,320]{1,0:T(1,128)}, u32[]{:S(2)}) copy-start(s32[1,320]{1,0:T(1,128)} %get-tuple-element.76.label_ref) | copy-start | bytes 3844
  58.8 26.4 %all-to-all-start.8 = ((f32[8,144,320]{2,1,0:T(8,128)}), f32[8,144,320]{2,1,0:T(8,128)S(1)}, u32[]{:S(2)}, u32[]{:S(2)}) async-start(f32[8,144,320]{2,1,0:T(8,128)} %broadcast_in_dim.43), calls=%async_computation.8 | async-start | bytes 3538944 | tf_op jit(solution)/shard_map/cond/branch_1_fun/all_to_all | solution.py:25
  122.0 28.7 %all-to-all-start.12 = ((bf16[16,48,128]{2,1,0:T(8,128)(2,1)}), bf16[16,48,128]{2,1,0:T(8,128)(2,1)S(1)}, u32[]{:S(2)}, u32[]{:S(2)}) async-start(bf16[16,48,128]{2,1,0:T(8,128)(2,1)} %reduce_sum.138), calls=%async_computation.12 | async-start | bytes 393216 | tf_op jit(solution)/shard_map/cond/branch_1_fun/all_to_all | solution.py:25
  137.8 4.0 %collective-permute-start.11 = (bf16[4,144,320]{2,1,0:T(8,128)(2,1)S(1)}, bf16[4,144,320]{2,1,0:T(8,128)(2,1)S(1)}, u32[]{:S(2)}, u32[]{:S(2)}) collective-permute-start(bf16[4,144,320]{2,1,0:T(8,128)(2,1)S(1)} %slice.154), channel_id=1, source_target_pairs={{0,8},{8,0},{1,9},{9,1},{2,10},{10,2},{3,11},{11,3},{4,12},{12,4},... | collective-permute-start | bytes 1105928 | tf_op jit(solution)/shard_map/cond/branch_1_fun/ppermute | solution.py:17
  141.9 30.6 %collective-permute-start.12 = (bf16[2,144,320]{2,1,0:T(8,128)(2,1)S(1)}, bf16[2,144,320]{2,1,0:T(8,128)(2,1)S(1)}, u32[]{:S(2)}, u32[]{:S(2)}) collective-permute-start(bf16[2,144,320]{2,1,0:T(8,128)(2,1)S(1)} %slice.241), channel_id=1, source_target_pairs={{0,512},{512,0},{1,513},{513,1},{2,514},{514,2},{3,515},{515,3},{4... | collective-permute-start | bytes 552968 | tf_op jit(solution)/shard_map/cond/branch_1_fun/ppermute | solution.py:17
  161.8 23.0 %all-to-all-start.14 = ((bf16[16,48,128]{2,1,0:T(8,128)(2,1)}), bf16[16,48,128]{2,1,0:T(8,128)(2,1)S(1)}, u32[]{:S(2)}, u32[]{:S(2)}) async-start(bf16[16,48,128]{2,1,0:T(8,128)(2,1)} %broadcast_in_dim.45), calls=%async_computation.14 | async-start | bytes 393216 | tf_op jit(solution)/shard_map/cond/branch_1_fun/all_to_all | solution.py:25
  172.5 9.9 %collective-permute-start.13 = (bf16[144,320]{1,0:T(8,128)(2,1)S(1)}, bf16[144,320]{1,0:T(8,128)(2,1)S(1)}, u32[]{:S(2)}, u32[]{:S(2)}) collective-permute-start(bf16[144,320]{1,0:T(8,128)(2,1)S(1)} %fusion.5), channel_id=1, source_target_pairs={{0,32},{32,0},{1,33},{33,1},{2,34},{34,2},{3,35},{35,3},{4,36},{36... | collective-permute-start | bytes 276488 | tf_op jit(solution)/shard_map/cond/branch_1_fun/ppermute | solution.py:17
  199.5 0.8 copy-start.10
  199.5 0.9 copy-start.11

commit v2 on v1

v2 whole, which is shorter than its diff:
```python
import jax
import jax.numpy as jnp
from jax import lax
from jax.experimental import pallas as pl
from jax.experimental.pallas import tpu as pltpu
from jax.sharding import Mesh
from jax.sharding import PartitionSpec as P

EPSILON = 1e-06
LANES = 128
ROW_TILE = 16
SWAP = [(0, 1), (1, 0)]
VMEM_LIMIT = 48 * 1024 * 1024
SMEM = pl.BlockSpec(memory_space=pltpu.SMEM)
VMEM = pl.BlockSpec(memory_space=pltpu.VMEM)


def swap(shard, axis):
    return lax.ppermute(shard, axis, SWAP)


def exchange(parts, axes):
    return lax.all_to_all(parts, axes, 0, 0, tiled=False)


def gather(shard, axes, count):
    return exchange(jnp.broadcast_to(shard[None], (count,) + shard.shape), axes)


def after(value, earlier):
    return lax.optimization_barrier((value, earlier))[0]


def low(value):
    return value.astype(jnp.bfloat16)


def wide(value):
    return value.astype(jnp.float32)


def summed(parts):
    return jnp.sum(wide(parts), axis=0)


def round_up(value, step):
    return -(-value // step) * step


def tile_kernel(number_ref, index_ref, label_ref, embed_ref, text_ref, out_ref):
    scale = number_ref[0]
    bias = number_ref[1]
    rows = label_ref.shape[1]
    width = embed_ref.shape[0] * embed_ref.shape[1] * 2
    halves = wide(embed_ref[...])
    embed = jnp.concatenate([halves[:, :, :rows], halves[:, :, rows:]], axis=1)
    embed = embed.reshape(width, rows)
    img_rinv = lax.rsqrt(jnp.sum(embed * embed, axis=0, keepdims=True) + EPSILON)
    img_unit = embed * img_rinv
    img_low = low(img_unit)
    halves = wide(text_ref[...])
    text = jnp.concatenate([halves[:, :, :rows], halves[:, :, rows:]], axis=1)
    text = text.reshape(width, rows)
    txt_rinv = lax.rsqrt(jnp.sum(text * text, axis=0, keepdims=True) + EPSILON)
    txt_unit = text * txt_rinv
    txt_low = low(txt_unit)
    score = lax.dot_general(
        txt_low, img_low, (((0,), (0,)), ((), ())), preferred_element_type=jnp.float32
    )
    logits = scale * score + bias
    text_ids = lax.broadcasted_iota(jnp.int32, score.shape, 0)
    own_text = jnp.where(index_ref[0] == 0, label_ref[...], -1)
    label_sign = jnp.where(text_ids == own_text, 1.0, -1.0).astype(jnp.float32)
    tile_grad = low(-label_sign * jax.nn.sigmoid(-label_sign * logits))
    img_dir = scale * jnp.dot(txt_low, tile_grad, preferred_element_type=jnp.float32)
    image_dot = jnp.sum(img_unit * img_dir, axis=0, keepdims=True)
    img_part = img_rinv * (img_dir - img_unit * image_dot)
    txt_dir = scale * lax.dot_general(
        img_low, tile_grad, (((1,), (1,)), ((), ())), preferred_element_type=jnp.float32
    )
    text_dot = jnp.sum(txt_unit * txt_dir, axis=0, keepdims=True)
    txt_part = txt_rinv * (txt_dir - txt_unit * text_dot)
    both = jnp.concatenate([img_part, txt_part], axis=1)
    cores, parts, half = out_ref.shape[:3]
    for part in range(parts):
        for core in range(cores):
            start = (part * cores + core) * half
            out_ref[core, part] = low(both[start : start + half])


def tile_parts(numbers, indices, labels, embed, text):
    rows = labels.shape[1]
    parts, half = text.shape[:2]
    return pl.pallas_call(
        tile_kernel,
        out_shape=jax.ShapeDtypeStruct((2, parts, half, 2 * rows), jnp.bfloat16),
        in_specs=[SMEM, SMEM, VMEM, VMEM, VMEM],
        out_specs=VMEM,
        compiler_params=pltpu.CompilerParams(vmem_limit_bytes=VMEM_LIMIT),
        name="tile_parts",
    )(numbers, indices, labels, embed, text)


def head_kernel(index_ref, part_ref, feats_ref, other_ref, out_ref, keep_ref, send_ref):
    own = index_ref[1]
    rows, width = feats_ref.shape
    own_grad = low(jnp.sum(wide(part_ref[own, :, :, :rows]), axis=0))
    other_grad = low(jnp.sum(wide(part_ref[1 - own, :, :, :rows]), axis=0))
    product = jnp.dot(own_grad, feats_ref[...], preferred_element_type=jnp.float32)
    product += jnp.dot(other_grad, other_ref[...], preferred_element_type=jnp.float32)
    blocks = [product[:, start : start + LANES] for start in range(0, width, LANES)]
    spare = out_ref.shape[0] - len(blocks) * product.shape[0]
    if spare:
        blocks.append(jnp.zeros((spare, LANES), jnp.float32))
    out_ref[...] = low(jnp.concatenate(blocks, axis=0))
    kept = keep_ref.shape[1]
    for core in range(2):
        for part in range(2 * kept):
            first = wide(part_ref[0, core * 2 * kept + part, :, rows:])
            second = wide(part_ref[1, (1 - core) * 2 * kept + part, :, rows:])
            if part % 2 == 0:
                keep_ref[core, part // 2] = first + second
            else:
                send_ref[core, part // 2] = low(first + second)


def head_rows(indices, parts, feats, other_feats, total_rows):
    half = parts.shape[2]
    kept = (2, parts.shape[1] // 4, half, feats.shape[0])
    return pl.pallas_call(
        head_kernel,
        out_shape=(
            jax.ShapeDtypeStruct((total_rows, LANES), jnp.bfloat16),
            jax.ShapeDtypeStruct(kept, jnp.float32),
            jax.ShapeDtypeStruct(kept, jnp.bfloat16),
        ),
        in_specs=[SMEM, VMEM, VMEM, VMEM],
        out_specs=(VMEM, VMEM, VMEM),
        compiler_params=pltpu.CompilerParams(vmem_limit_bytes=VMEM_LIMIT),
        name="head_rows",
    )(indices, parts, feats, other_feats)


def unpack_kernel(index_ref, own_ref, other_ref, out_ref):
    own = index_ref[1]
    half = out_ref.shape[1]
    own_rows, other_rows = wide(own_ref[...]), wide(other_ref[...])
    for block in range(out_ref.shape[2] // LANES):
        columns = slice(block * LANES, (block + 1) * LANES)
        rows = slice(block * half, (block + 1) * half)
        out_ref[own, :, columns] = own_rows[rows]
        out_ref[1 - own, :, columns] = other_rows[rows]


def unpacked(indices, own, other, half, width):
    return pl.pallas_call(
        unpack_kernel,
        out_shape=jax.ShapeDtypeStruct((2, half, width), jnp.float32),
        in_specs=[SMEM, VMEM, VMEM],
        out_specs=VMEM,
        compiler_params=pltpu.CompilerParams(vmem_limit_bytes=VMEM_LIMIT),
        name="unpacked",
    )(indices, own, other)


def solution(mesh):
    dp, mp = mesh.shape["dp"], mesh.shape["mp"]
    bits = dp.bit_length() - 1
    names = tuple(f"b{bit}" for bit in reversed(range(bits)))
    wide_mp, pair = "x", "y"
    mp_names = (wide_mp, pair)
    fine = Mesh(mesh.devices.reshape((2,) * bits + (mp // 2, 2)), names + mp_names)
    core, top = "b0", names[0]
    far, near = names[:2], names[2:-1]
    near_count, far_count = 2 ** len(near), 2 ** len(far)

    def with_middle(middle, feats, weight, text, scale, bias, labels):
        share, width = weight.shape
        half = share // 2
        rows = feats.shape[0]
        core_index = lax.axis_index(core).astype(jnp.int32)
        mp_index = lax.axis_index(mp_names).astype(jnp.int32)
        indices = jnp.stack([mp_index, core_index])
        numbers = jnp.concatenate([scale, bias])
        own = text.T
        own = jnp.concatenate([own[:half], own[half:]], axis=1)
        two = jnp.stack([own, swap(own, middle)])
        four = jnp.concatenate([two, swap(two, top)])
        eight = jnp.concatenate([four, swap(four, core)])
        other_feats = swap(feats, core)
        embedding = lax.dot_general(
            weight, feats, (((1,), (1,)), ((), ())), preferred_element_type=jnp.float32
        )
        embedding = gather(jnp.concatenate([embedding[:half], embedding[half:]], axis=1), mp_names, mp)
        met_text = exchange(after(eight, embedding), mp_names)
        parts = tile_parts(numbers, indices, labels, embedding, met_text)
        parts = after(parts, other_feats)
        parts = exchange(parts.reshape((2 * mp,) + parts.shape[2:]), (core,) + mp_names)
        parts = parts.reshape(2, mp, half, 2 * rows)
        used_rows = half * width // LANES
        head, kept, sent = head_rows(
            indices, parts, feats, other_feats, round_up(used_rows, near_count * ROW_TILE)
        )
        head = summed(exchange(head.reshape(near_count, -1, LANES), near))
        back = swap(sent, middle)
        head = low(summed(gather(head, far, far_count)))
        head = after(head, back)
        txt = kept + wide(back)
        back = swap(low(txt[:, 1]), top)
        head = gather(head, near, near_count)
        head = after(head, back)
        txt = txt[:, 0] + wide(back)
        is_first = core_index == 0
        own_txt = jnp.where(is_first, txt[0], txt[1])
        back = swap(jnp.where(is_first, txt[1], txt[0]), core)
        text_grad = jnp.concatenate(
            [jnp.where(is_first, own_txt, back), jnp.where(is_first, back, own_txt)]
        ).T
        head = head.reshape(-1, LANES)
        head = unpacked(indices, head, swap(head, core), half, width)
        return head.reshape(share, width), text_grad

    def on_device(feats, weight, text, scale, bias, labels, plan):
        middle_bit = jnp.max(jnp.where(plan == bits - 1, 0, plan))
        branches = [
            (lambda *args, name=f"b{bit}": with_middle(name, *args)) for bit in range(1, bits - 1)
        ]
        return lax.switch(middle_bit - 1, branches, feats, weight, text, scale, bias, labels)

    return jax.shard_map(
        on_device,
        mesh=fine,
        in_specs=(
            P(names, None),
            P(mp_names, None),
            P(names, mp_names),
            P(),
            P(),
            P(names, None),
            P(),
        ),
        out_specs=(P(mp_names, None), P(names, mp_names)),
        check_vma=False,
    )
```

time: 201 us -> 171 us (0.85)
  blocking collectives: 56.1 us -> 23.7 us
  starting transfers between devices: 66.3 us -> 85 us
  waiting for transfers between devices: 59.1 us -> 43.7 us
  local copies, waits for them, and re-layouts: 7.57 us -> 2.61 us
  Pallas kernels: 4.17 us -> 7.01 us
    all_to_all x4 -> x1, blocking collectives: 56.1 us -> 23.7 us  [exchange(): return lax.all_to_all(parts, axes, 0, 0, tiled=False)]
    all_to_all x4 -> x5, waiting for transfers between devices: 43.1 us -> 18.9 us  [exchange(): return lax.all_to_all(parts, axes, 0, 0, tiled=False)]
    ppermute x6 -> x8, waiting for transfers between devices: 7.1 us -> 24.8 us  [swap(): return lax.ppermute(shard, axis, SWAP)]
    ppermute x6 -> x8, starting transfers between devices: 30.7 us -> 45 us  [swap(): return lax.ppermute(shard, axis, SWAP)]
    ppermute x1 -> x0, waiting for transfers between devices: 8.89 us -> none  [swap_both(): return lax.ppermute(shard, (first, second), [(i, i ^ 3) for i in range(4)])]
    all_to_all x4 -> x5, starting transfers between devices: 33.7 us -> 40 us  [exchange(): return lax.all_to_all(parts, axes, 0, 0, tiled=False)]
    unnamed x14 -> x0, local copies, waits for them, and re-layouts: 4.43 us -> none
    pallas_call x2 -> x3, Pallas kernels: 4.17 us -> 7.01 us  [the longest x1 3.85 us: tile_parts(): pl.pallas_call(tile_kernel, out_shape=jax.ShapeDtypeStruct((2, parts, hal...]
  transfers between devices with their start and end apart: 11 -> 13, of which waited for: 7 -> 9; matrix products, arithmetic and copies ran while one was open for 3% -> 2% of each run, Pallas kernels for 0% -> 2%
where the time goes in v2:
time: 171 us; the launch traced here: 170 us
  starting transfers between devices  85 us (50%)
  waiting for transfers between devices  43.7 us (26%)
  blocking collectives  23.7 us (14%)
  Pallas kernels  7.01 us (4%)
  other arithmetic  4.88 us (3%)
  local copies, waits for them, and re-layouts  2.61 us (2%)
    ppermute x8, starting transfers between devices, swap(): return lax.ppermute(shard, axis, SWAP)  45 us
    all_to_all x5, starting transfers between devices, exchange(): return lax.all_to_all(parts, axes, 0, 0, tiled=False)  40 us
    ppermute x8, waiting for transfers between devices, swap(): return lax.ppermute(shard, axis, SWAP)  24.8 us
    all_to_all x1, blocking collectives, exchange(): return lax.all_to_all(parts, axes, 0, 0, tiled=False)  23.7 us
    all_to_all x5, waiting for transfers between devices, exchange(): return lax.all_to_all(parts, axes, 0, 0, tiled=False)  18.9 us
    pallas_call x1, Pallas kernels, tile_parts(): pl.pallas_call(tile_kernel, out_shape=jax.ShapeDtypeStruct((2, parts, hal...  3.85 us
  transfers between devices with their start and end apart: 13, of which 9 were waited for; matrix products, arithmetic and copies ran while one was open for 2% of the time, Pallas kernels for 2%

profile of v2, /device:TPU:1, one launch (start us, length us, event | category | flops | bytes accessed | tf_op | source)
XLA Modules:
  0.0 170.1 jit_solution(3934851801587384053)
XLA Ops:
  0.6 1.3 fusion.10
  2.6 167.5 %conditional.1 = (f32[144,1152]{1,0:T(8,128)}, f32[320,144]{0,1:T(8,128)}) conditional(s32[]{:T(128)} %clamp.3, (f32[1]{0:T(128)}, f32[1]{0:T(128)}, bf16[144,1152]{1,0:T(8,128)(2,1)}, bf16[320,1152]{1,0:T(8,128)(2,1)}, bf16[320,144]{0,1:T(8,128)(2,1)}, /*index=5*/s32[1,320]{1,0:T(1,128)}) %tuple.47, (f32[1]{0:T(128)}, ...), branch_computations={%region_1.4_spmd, %region_4.7_spmd, %region_7.10_spmd, %region_10.... | conditional | flops 108773392 | bytes 32312028 | solution.py:228
  2.6 1.6 fusion.22
  4.3 0.1 pad_maximum_fusion.8
  4.4 1.2 broadcast_in_dim.33
  5.6 6.0 %all-to-all-start.6 = ((f32[8,72,640]{2,1,0:T(8,128)}), f32[8,72,640]{2,1,0:T(8,128)S(1)}, u32[]{:S(2)}, u32[]{:S(2)}) async-start(f32[8,72,640]{2,1,0:T(8,128)} %broadcast_in_dim.33), calls=%async_computation.6 | async-start | bytes 2949120 | tf_op jit(solution)/shard_map/cond/branch_1_fun/all_to_all | solution.py:23
  11.6 0.0 copy-done.6
  11.6 0.1 pad_maximum_fusion.10
  11.7 5.8 %collective-permute-start.8 = (bf16[72,640]{1,0:T(8,128)(2,1)S(1)}, bf16[72,640]{1,0:T(8,128)(2,1)S(1)}, u32[]{:S(2)}, u32[]{:S(2)}) collective-permute-start(bf16[72,640]{1,0:T(8,128)(2,1)S(1)} %pad_maximum_fusion.10), channel_id=1, source_target_pairs={{0,32},{32,0},{1,33},{33,1},{2,34},{34,2},{3,35},{35,3},{4,36},{36... | collective-permute-start | bytes 276488 | tf_op jit(solution)/shard_map/cond/branch_1_fun/ppermute | solution.py:19
  17.5 0.1 fusion.37
  17.6 1.8 %collective-permute-done.8 = bf16[72,640]{1,0:T(8,128)(2,1)S(1)} collective-permute-done((bf16[72,640]{1,0:T(8,128)(2,1)S(1)}, bf16[72,640]{1,0:T(8,128)(2,1)S(1)}, u32[]{:S(2)}, u32[]{:S(2)}) %collective-permute-start.8) | collective-permute-done | bytes 92192 | tf_op jit(solution)/shard_map/cond/branch_1_fun/ppermute | solution.py:19
  19.5 6.8 %collective-permute-start.9 = (bf16[2,72,640]{2,1,0:T(8,128)(2,1)S(1)}, bf16[2,72,640]{2,1,0:T(8,128)(2,1)S(1)}, u32[]{:S(2)}, u32[]{:S(2)}) collective-permute-start(bf16[2,72,640]{2,1,0:T(8,128)(2,1)S(1)} %pad_maximum_fusion.9), channel_id=1, source_target_pairs={{0,512},{512,0},{1,513},{513,1},{2,514},{514,2},{3,515},{515,3},{4... | collective-permute-start | bytes 552968 | tf_op jit(solution)/shard_map/cond/branch_1_fun/ppermute | solution.py:19
  26.3 9.7 %collective-permute-done.9 = bf16[2,72,640]{2,1,0:T(8,128)(2,1)S(1)} collective-permute-done((bf16[2,72,640]{2,1,0:T(8,128)(2,1)S(1)}, bf16[2,72,640]{2,1,0:T(8,128)(2,1)S(1)}, u32[]{:S(2)}, u32[]{:S(2)}) %collective-permute-start.9) | collective-permute-done | bytes 184352 | tf_op jit(solution)/shard_map/cond/branch_1_fun/ppermute | solution.py:19
  36.1 0.0 copy-start.11
  36.1 8.4 %collective-permute-start.10 = (bf16[4,72,640]{2,1,0:T(8,128)(2,1)S(1)}, bf16[4,72,640]{2,1,0:T(8,128)(2,1)S(1)}, u32[]{:S(2)}, u32[]{:S(2)}) collective-permute-start(bf16[4,72,640]{2,1,0:T(8,128)(2,1)S(1)} %pad_maximum_fusion.7), channel_id=1, source_target_pairs={{0,8},{8,0},{1,9},{9,1},{2,10},{10,2},{3,11},{11,3},{4,12},{12,4},... | collective-permute-start | bytes 1105928 | tf_op jit(solution)/shard_map/cond/branch_1_fun/ppermute | solution.py:19
  44.5 1.3 collective-permute-done.10
  45.8 1.0 pad_maximum_fusion.6
  46.8 0.0 all-to-all-done.6.embed_ref
  46.8 5.1 %all-to-all-start.7 = ((bf16[8,72,640]{2,1,0:T(8,128)(2,1)}), bf16[8,72,640]{2,1,0:T(8,128)(2,1)S(1)}, u32[]{:S(2)}, u32[]{:S(2)}) async-start(bf16[8,72,640]{2,1,0:T(8,128)(2,1)} %pad_maximum_fusion.6), calls=%async_computation.7 | async-start | bytes 1474560 | tf_op jit(solution)/shard_map/cond/branch_1_fun/all_to_all | solution.py:23
  51.8 2.6 %collective-permute-start.11 = (bf16[320,1152]{1,0:T(8,128)(2,1)}, bf16[320,1152]{1,0:T(8,128)(2,1)S(1)}, u32[]{:S(2)}, u32[]{:S(2)}) collective-permute-start(bf16[320,1152]{1,0:T(8,128)(2,1)} %get-tuple-element.77.feats_ref), channel_id=1, source_target_pairs={{0,8},{8,0},{1,9},{9,1},{2,10},{10,2},{3,11},{11,3},{4,12},{12,4},... | collective-permute-start | bytes 2211848 | tf_op jit(solution)/shard_map/cond/branch_1_fun/ppermute | solution.py:19
  54.4 0.1 pad_add_fusion.1.index_ref
  54.5 1.4 pad_maximum_fusion.11.number_ref
  55.9 7.5 %all-to-all-done.7.text_ref = bf16[8,72,640]{2,1,0:T(8,128)(2,1)S(1)} async-done(((bf16[8,72,640]{2,1,0:T(8,128)(2,1)}), bf16[8,72,640]{2,1,0:T(8,128)(2,1)S(1)}, u32[]{:S(2)}, u32[]{:S(2)}) %all-to-all-start.7) | async-done | bytes 737312 | tf_op jit(solution)/shard_map/cond/branch_1_fun/all_to_all | solution.py:23
  63.3 0.0 copy-done.11
  63.3 3.9 %tile_parts.6 = bf16[2,8,72,640]{3,2,1,0:T(8,128)(2,1)S(1)} custom-call(f32[2]{0:T(128)S(1)} %pad_maximum_fusion.11.number_ref, s32[2]{0:T(128)S(1)} %pad_add_fusion.1.index_ref, s32[1,320]{1,0:T(1,128)S(1)} %copy-done.11, f32[8,72,640]{2,1,0:T(8,128)S(1)} %all-to-all-done.6.embed_ref, bf16[8,72,640]{2,1,0:T(8,128)(2,1)S(1)} %all-to-all-done.7.text_ref), custom_call_target="tpu_custom_call" | custom-call | tf_op jit(solution)/shard_map/cond/branch_1_fun/tile_parts/pallas_call | solution.py:94
  67.2 0.0 collective-permute-done.11.other_ref
  67.2 0.0 copy-start.1
  67.2 23.7 %all_to_all.121 = bf16[16,72,640]{2,1,0:T(8,128)(2,1)S(1)} all-to-all(bf16[16,72,640]{2,1,0:T(8,128)(2,1)S(1)} %bitcast.131), channel_id=1, replica_groups=mesh['b6'=2,'b5'=2,'b4'=2,'b3'=2,'b2'=2,'b1'=2,'b0'=2,'x'=4,'y'=2] {'b0'..., dimensions={0} | all-to-all | bytes 2949120 | tf_op jit(solution)/shard_map/cond/branch_1_fun/all_to_all | solution.py:23
  91.0 0.0 copy-done.1
  91.0 1.7 %head_rows.6 = (bf16[768,128]{1,0:T(8,128)(2,1)}, f32[2,2,72,320]{3,2,1,0:T(8,128)S(1)}, bf16[2,2,72,320]{3,2,1,0:T(8,128)(2,1)S(1)}) custom-call(s32[2]{0:T(128)S(1)} %pad_add_fusion.1.index_ref, bf16[2,8,72,640]{3,2,1,0:T(8,128)(2,1)S(1)} %bitcast.136, bf16[320,1152]{1,0:T(8,128)(2,1)S(1)} %copy-done.1, bf16[320,1152]{1,0:T(8,128)(2,1)S(1)} %collective-permute-done.11.other_ref), custom_call_target="tpu_custom_call" | custom-call | tf_op jit(solution)/shard_map/cond/branch_1_fun/head_rows/pallas_call | solution.py:130
  92.7 18.2 %all-to-all-start.9 = ((bf16[16,48,128]{2,1,0:T(8,128)(2,1)}), bf16[16,48,128]{2,1,0:T(8,128)(2,1)S(1)}, u32[]{:S(2)}, u32[]{:S(2)}) async-start(bf16[16,48,128]{2,1,0:T(8,128)(2,1)} %bitcast.22), calls=%async_computation.9 | async-start | bytes 393216 | tf_op jit(solution)/shard_map/cond/branch_1_fun/all_to_all | solution.py:23
  110.9 4.2 %collective-permute-start.12 = (bf16[2,2,72,320]{3,2,1,0:T(8,128)(2,1)S(1)}, bf16[2,2,72,320]{3,2,1,0:T(8,128)(2,1)S(1)}, u32[]{:S(2)}, u32[]{:S(2)}) collective-permute-start(bf16[2,2,72,320]{3,2,1,0:T(8,128)(2,1)S(1)} %get-tuple-element.82), channel_id=1, source_target_pairs={{0,32},{32,0},{1,33},{33,1},{2,34},{34,2},{3,35},{35,3},{4,36},{36... | collective-permute-start | bytes 552968 | tf_op jit(solution)/shard_map/cond/branch_1_fun/ppermute | solution.py:19
  115.1 8.2 %all-to-all-done.9 = bf16[16,48,128]{2,1,0:T(8,128)(2,1)S(1)} async-done(((bf16[16,48,128]{2,1,0:T(8,128)(2,1)}), bf16[16,48,128]{2,1,0:T(8,128)(2,1)S(1)}, u32[]{:S(2)}, u32[]{:S(2)}) %all-to-all-start.9) | async-done | bytes 196640 | tf_op jit(solution)/shard_map/cond/branch_1_fun/all_to_all | solution.py:23
  123.3 0.6 broadcast_in_dim.34
  123.9 3.3 %all-to-all-start.10 = ((f32[4,48,128]{2,1,0:T(8,128)}), f32[4,48,128]{2,1,0:T(8,128)S(1)}, u32[]{:S(2)}, u32[]{:S(2)}) async-start(f32[4,48,128]{2,1,0:T(8,128)} %broadcast_in_dim.34), calls=%async_computation.10 | async-start | bytes 196608 | tf_op jit(solution)/shard_map/cond/branch_1_fun/all_to_all | solution.py:23
  127.3 4.0 %collective-permute-done.12 = bf16[2,2,72,320]{3,2,1,0:T(8,128)(2,1)S(1)} collective-permute-done((bf16[2,2,72,320]{3,2,1,0:T(8,128)(2,1)S(1)}, bf16[2,2,72,320]{3,2,1,0:T(8,128)(2,1)S(1)}, u32[]{:S(2)}, u32[]{:S(2)}) %collective-permute-start.12) | collective-permute-done | bytes 184352 | tf_op jit(solution)/shard_map/cond/branch_1_fun/ppermute | solution.py:19
  131.3 3.2 %all-to-all-done.10 = f32[4,48,128]{2,1,0:T(8,128)S(1)} async-done(((f32[4,48,128]{2,1,0:T(8,128)}), f32[4,48,128]{2,1,0:T(8,128)S(1)}, u32[]{:S(2)}, u32[]{:S(2)}) %all-to-all-start.10) | async-done | bytes 98336 | tf_op jit(solution)/shard_map/cond/branch_1_fun/all_to_all | solution.py:23
  134.5 0.7 broadcast_in_dim.35
  135.2 7.4 %all-to-all-start.11 = ((bf16[16,48,128]{2,1,0:T(8,128)(2,1)}), bf16[16,48,128]{2,1,0:T(8,128)(2,1)S(1)}, u32[]{:S(2)}, u32[]{:S(2)}) async-start(bf16[16,48,128]{2,1,0:T(8,128)(2,1)} %broadcast_in_dim.35), calls=%async_computation.11 | async-start | bytes 393216 | tf_op jit(solution)/shard_map/cond/branch_1_fun/all_to_all | solution.py:23
  142.7 2.2 %collective-permute-start.13 = (bf16[2,72,320]{2,1,0:T(8,128)(2,1)S(1)}, bf16[2,72,320]{2,1,0:T(8,128)(2,1)S(1)}, u32[]{:S(2)}, u32[]{:S(2)}) collective-permute-start(bf16[2,72,320]{2,1,0:T(8,128)(2,1)S(1)} %fusion.3), channel_id=1, source_target_pairs={{0,512},{512,0},{1,513},{513,1},{2,514},{514,2},{3,515},{515,3},{4... | collective-permute-start | bytes 276488 | tf_op jit(solution)/shard_map/cond/branch_1_fun/ppermute | solution.py:19
  144.9 7.3 %collective-permute-done.13 = bf16[2,72,320]{2,1,0:T(8,128)(2,1)S(1)} collective-permute-done((bf16[2,72,320]{2,1,0:T(8,128)(2,1)S(1)}, bf16[2,72,320]{2,1,0:T(8,128)(2,1)S(1)}, u32[]{:S(2)}, u32[]{:S(2)}) %collective-permute-start.13) | collective-permute-done | bytes 92192 | tf_op jit(solution)/shard_map/cond/branch_1_fun/ppermute | solution.py:19
  152.2 13.1 %collective-permute-start.15 = (f32[72,320]{1,0:T(8,128)S(1)}, f32[72,320]{1,0:T(8,128)S(1)}, u32[]{:S(2)}, u32[]{:S(2)}) collective-permute-start(f32[72,320]{1,0:T(8,128)S(1)} %select_bitcast_fusion.1), channel_id=1, source_target_pairs={{0,8},{8,0},{1,9},{9,1},{2,10},{10,2},{3,11},{11,3},{4,12},{12,4},... | collective-permute-start | bytes 276488 | tf_op jit(solution)/shard_map/cond/branch_1_fun/ppermute | solution.py:19
  165.3 0.0 all-to-all-done.11
  165.3 1.9 %collective-permute-start.14 = (bf16[768,128]{1,0:T(8,128)(2,1)S(1)}, bf16[768,128]{1,0:T(8,128)(2,1)S(1)}, u32[]{:S(2)}, u32[]{:S(2)}) collective-permute-start(bf16[768,128]{1,0:T(8,128)(2,1)S(1)} %bitcast.142), channel_id=1, source_target_pairs={{0,8},{8,0},{1,9},{9,1},{2,10},{10,2},{3,11},{11,3},{4,12},{12,4},... | collective-permute-start | bytes 589832 | tf_op jit(solution)/shard_map/cond/branch_1_fun/ppermute | solution.py:19
  167.3 0.0 collective-permute-done.15
  167.3 0.7 maximum_bitcast_fusion.1
  168.0 0.7 collective-permute-done.14.other_ref
  168.7 1.4 unpacked.6
  (12 shorter events, 0.3 us)
Async XLA Ops:
  5.6 6.0 %copy-start.6 = (bf16[320,144]{0,1:T(8,128)(2,1)S(1)}, bf16[320,144]{0,1:T(8,128)(2,1)}, u32[]{:S(2)}) copy-start(bf16[320,144]{0,1:T(8,128)(2,1)} %get-tuple-element.78) | copy-start | bytes 276484 | tf_op jit(solution)/shard_map/cond
  5.6 41.2 %all-to-all-start.6 = ((f32[8,72,640]{2,1,0:T(8,128)}), f32[8,72,640]{2,1,0:T(8,128)S(1)}, u32[]{:S(2)}, u32[]{:S(2)}) async-start(f32[8,72,640]{2,1,0:T(8,128)} %broadcast_in_dim.33), calls=%async_computation.6 | async-start | bytes 2949120 | tf_op jit(solution)/shard_map/cond/branch_1_fun/all_to_all | solution.py:23
  11.7 7.7 %collective-permute-start.8 = (bf16[72,640]{1,0:T(8,128)(2,1)S(1)}, bf16[72,640]{1,0:T(8,128)(2,1)S(1)}, u32[]{:S(2)}, u32[]{:S(2)}) collective-permute-start(bf16[72,640]{1,0:T(8,128)(2,1)S(1)} %pad_maximum_fusion.10), channel_id=1, source_target_pairs={{0,32},{32,0},{1,33},{33,1},{2,34},{34,2},{3,35},{35,3},{4,36},{36... | collective-permute-start | bytes 276488 | tf_op jit(solution)/shard_map/cond/branch_1_fun/ppermute | solution.py:19
  19.5 16.6 %collective-permute-start.9 = (bf16[2,72,640]{2,1,0:T(8,128)(2,1)S(1)}, bf16[2,72,640]{2,1,0:T(8,128)(2,1)S(1)}, u32[]{:S(2)}, u32[]{:S(2)}) collective-permute-start(bf16[2,72,640]{2,1,0:T(8,128)(2,1)S(1)} %pad_maximum_fusion.9), channel_id=1, source_target_pairs={{0,512},{512,0},{1,513},{513,1},{2,514},{514,2},{3,515},{515,3},{4... | collective-permute-start | bytes 552968 | tf_op jit(solution)/shard_map/cond/branch_1_fun/ppermute | solution.py:19
  36.1 27.3 %copy-start.11 = (s32[1,320]{1,0:T(1,128)S(1)}, s32[1,320]{1,0:T(1,128)}, u32[]{:S(2)}) copy-start(s32[1,320]{1,0:T(1,128)} %get-tuple-element.75.label_ref) | copy-start | bytes 3844 | tf_op jit(solution)/shard_map/cond
  36.1 9.7 %collective-permute-start.10 = (bf16[4,72,640]{2,1,0:T(8,128)(2,1)S(1)}, bf16[4,72,640]{2,1,0:T(8,128)(2,1)S(1)}, u32[]{:S(2)}, u32[]{:S(2)}) collective-permute-start(bf16[4,72,640]{2,1,0:T(8,128)(2,1)S(1)} %pad_maximum_fusion.7), channel_id=1, source_target_pairs={{0,8},{8,0},{1,9},{9,1},{2,10},{10,2},{3,11},{11,3},{4,12},{12,4},... | collective-permute-start | bytes 1105928 | tf_op jit(solution)/shard_map/cond/branch_1_fun/ppermute | solution.py:19
  46.8 16.6 %all-to-all-start.7 = ((bf16[8,72,640]{2,1,0:T(8,128)(2,1)}), bf16[8,72,640]{2,1,0:T(8,128)(2,1)S(1)}, u32[]{:S(2)}, u32[]{:S(2)}) async-start(bf16[8,72,640]{2,1,0:T(8,128)(2,1)} %pad_maximum_fusion.6), calls=%async_computation.7 | async-start | bytes 1474560 | tf_op jit(solution)/shard_map/cond/branch_1_fun/all_to_all | solution.py:23
  51.8 15.4 %collective-permute-start.11 = (bf16[320,1152]{1,0:T(8,128)(2,1)}, bf16[320,1152]{1,0:T(8,128)(2,1)S(1)}, u32[]{:S(2)}, u32[]{:S(2)}) collective-permute-start(bf16[320,1152]{1,0:T(8,128)(2,1)} %get-tuple-element.77.feats_ref), channel_id=1, source_target_pairs={{0,8},{8,0},{1,9},{9,1},{2,10},{10,2},{3,11},{11,3},{4,12},{12,4},... | collective-permute-start | bytes 2211848 | tf_op jit(solution)/shard_map/cond/branch_1_fun/ppermute | solution.py:19
  67.2 23.7 %copy-start.1 = (bf16[320,1152]{1,0:T(8,128)(2,1)S(1)}, bf16[320,1152]{1,0:T(8,128)(2,1)}, u32[]{:S(2)}) copy-start(bf16[320,1152]{1,0:T(8,128)(2,1)} %get-tuple-element.77.feats_ref) | copy-start | bytes 2211844 | tf_op jit(solution)/shard_map/cond
  92.7 30.6 %all-to-all-start.9 = ((bf16[16,48,128]{2,1,0:T(8,128)(2,1)}), bf16[16,48,128]{2,1,0:T(8,128)(2,1)S(1)}, u32[]{:S(2)}, u32[]{:S(2)}) async-start(bf16[16,48,128]{2,1,0:T(8,128)(2,1)} %bitcast.22), calls=%async_computation.9 | async-start | bytes 393216 | tf_op jit(solution)/shard_map/cond/branch_1_fun/all_to_all | solution.py:23
  110.9 20.3 %collective-permute-start.12 = (bf16[2,2,72,320]{3,2,1,0:T(8,128)(2,1)S(1)}, bf16[2,2,72,320]{3,2,1,0:T(8,128)(2,1)S(1)}, u32[]{:S(2)}, u32[]{:S(2)}) collective-permute-start(bf16[2,2,72,320]{3,2,1,0:T(8,128)(2,1)S(1)} %get-tuple-element.82), channel_id=1, source_target_pairs={{0,32},{32,0},{1,33},{33,1},{2,34},{34,2},{3,35},{35,3},{4,36},{36... | collective-permute-start | bytes 552968 | tf_op jit(solution)/shard_map/cond/branch_1_fun/ppermute | solution.py:19
  123.9 10.6 %all-to-all-start.10 = ((f32[4,48,128]{2,1,0:T(8,128)}), f32[4,48,128]{2,1,0:T(8,128)S(1)}, u32[]{:S(2)}, u32[]{:S(2)}) async-start(f32[4,48,128]{2,1,0:T(8,128)} %broadcast_in_dim.34), calls=%async_computation.10 | async-start | bytes 196608 | tf_op jit(solution)/shard_map/cond/branch_1_fun/all_to_all | solution.py:23
  135.2 30.1 %all-to-all-start.11 = ((bf16[16,48,128]{2,1,0:T(8,128)(2,1)}), bf16[16,48,128]{2,1,0:T(8,128)(2,1)S(1)}, u32[]{:S(2)}, u32[]{:S(2)}) async-start(bf16[16,48,128]{2,1,0:T(8,128)(2,1)} %broadcast_in_dim.35), calls=%async_computation.11 | async-start | bytes 393216 | tf_op jit(solution)/shard_map/cond/branch_1_fun/all_to_all | solution.py:23
  142.7 9.5 %collective-permute-start.13 = (bf16[2,72,320]{2,1,0:T(8,128)(2,1)S(1)}, bf16[2,72,320]{2,1,0:T(8,128)(2,1)S(1)}, u32[]{:S(2)}, u32[]{:S(2)}) collective-permute-start(bf16[2,72,320]{2,1,0:T(8,128)(2,1)S(1)} %fusion.3), channel_id=1, source_target_pairs={{0,512},{512,0},{1,513},{513,1},{2,514},{514,2},{3,515},{515,3},{4... | collective-permute-start | bytes 276488 | tf_op jit(solution)/shard_map/cond/branch_1_fun/ppermute | solution.py:19
  152.2 15.0 %collective-permute-start.15 = (f32[72,320]{1,0:T(8,128)S(1)}, f32[72,320]{1,0:T(8,128)S(1)}, u32[]{:S(2)}, u32[]{:S(2)}) collective-permute-start(f32[72,320]{1,0:T(8,128)S(1)} %select_bitcast_fusion.1), channel_id=1, source_target_pairs={{0,8},{8,0},{1,9},{9,1},{2,10},{10,2},{3,11},{11,3},{4,12},{12,4},... | collective-permute-start | bytes 276488 | tf_op jit(solution)/shard_map/cond/branch_1_fun/ppermute | solution.py:19
  165.3 3.3 %collective-permute-start.14 = (bf16[768,128]{1,0:T(8,128)(2,1)S(1)}, bf16[768,128]{1,0:T(8,128)(2,1)S(1)}, u32[]{:S(2)}, u32[]{:S(2)}) collective-permute-start(bf16[768,128]{1,0:T(8,128)(2,1)S(1)} %bitcast.142), channel_id=1, source_target_pairs={{0,8},{8,0},{1,9},{9,1},{2,10},{10,2},{3,11},{11,3},{4,12},{12,4},... | collective-permute-start | bytes 589832 | tf_op jit(solution)/shard_map/cond/branch_1_fun/ppermute | solution.py:19

commit v3 on v2

--- a/solution.py
+++ b/solution.py
@@ -1,3 +1,5 @@
+from functools import partial
+
 import jax
 import jax.numpy as jnp
 from jax import lax
@@ -101,7 +103,7 @@
     )(numbers, indices, labels, embed, text)
 
 
-def head_kernel(index_ref, part_ref, feats_ref, other_ref, out_ref, keep_ref, send_ref):
+def head_kernel(by_last, index_ref, part_ref, feats_ref, other_ref, out_ref, keep_ref, send_ref):
     own = index_ref[1]
     rows, width = feats_ref.shape
     own_grad = low(jnp.sum(wide(part_ref[own, :, :, :rows]), axis=0))
@@ -118,17 +120,18 @@
         for part in range(2 * kept):
             first = wide(part_ref[0, core * 2 * kept + part, :, rows:])
             second = wide(part_ref[1, (1 - core) * 2 * kept + part, :, rows:])
-            if part % 2 == 0:
-                keep_ref[core, part // 2] = first + second
+            group, place = (part // 2, part % 2) if by_last else (part % kept, part // kept)
+            if place == 0:
+                keep_ref[core, group] = first + second
             else:
-                send_ref[core, part // 2] = low(first + second)
-
-
-def head_rows(indices, parts, feats, other_feats, total_rows):
+                send_ref[core, group] = low(first + second)
+
+
+def head_rows(indices, parts, feats, other_feats, total_rows, by_last):
     half = parts.shape[2]
     kept = (2, parts.shape[1] // 4, half, feats.shape[0])
     return pl.pallas_call(
-        head_kernel,
+        partial(head_kernel, by_last),
         out_shape=(
             jax.ShapeDtypeStruct((total_rows, LANES), jnp.bfloat16),
             jax.ShapeDtypeStruct(kept, jnp.float32),
@@ -141,6 +144,43 @@
     )(indices, parts, feats, other_feats)
 
 
+def fold_kernel(kept_ref, back_ref, keep_ref, send_ref):
+    keep_ref[...] = kept_ref[:, 0] + wide(back_ref[:, 0])
+    send_ref[...] = low(kept_ref[:, 1] + wide(back_ref[:, 1]))
+
+
+def folded(kept, back):
+    shape = kept.shape[:1] + kept.shape[2:]
+    return pl.pallas_call(
+        fold_kernel,
+        out_shape=(
+            jax.ShapeDtypeStruct(shape, jnp.float32),
+            jax.ShapeDtypeStruct(shape, jnp.bfloat16),
+        ),
+        in_specs=[VMEM, VMEM],
+        out_specs=(VMEM, VMEM),
+        name="folded",
+    )(kept, back)
+
+
+def finish_kernel(index_ref, kept_ref, back_ref, own_ref, other_ref):
+    own = index_ref[1]
+    own_ref[...] = kept_ref[own] + wide(back_ref[own])
+    other_ref[...] = kept_ref[1 - own] + wide(back_ref[1 - own])
+
+
+def finished(indices, kept, back):
+    shape = jax.ShapeDtypeStruct(kept.shape[1:], jnp.float32)
+    return pl.pallas_call(
+        finish_kernel,
+        out_shape=(shape, shape),
+        in_specs=[SMEM, VMEM, VMEM],
+        out_specs=(VMEM, VMEM),
+        cost_estimate=pl.CostEstimate(flops=10**11, bytes_accessed=10**8, transcendentals=0),
+        name="finished",
+    )(indices, kept, back)
+
+
 def unpack_kernel(index_ref, own_ref, other_ref, out_ref):
     own = index_ref[1]
     half = out_ref.shape[1]
@@ -172,6 +212,7 @@
     fine = Mesh(mesh.devices.reshape((2,) * bits + (mp // 2, 2)), names + mp_names)
     core, top = "b0", names[0]
     far, near = names[:2], names[2:-1]
+    slow = near[:2]
     near_count, far_count = 2 ** len(near), 2 ** len(far)
 
     def with_middle(middle, feats, weight, text, scale, bias, labels):
@@ -199,20 +240,36 @@
         parts = parts.reshape(2, mp, half, 2 * rows)
         used_rows = half * width // LANES
         head, kept, sent = head_rows(
-            indices, parts, feats, other_feats, round_up(used_rows, near_count * ROW_TILE)
+            indices,
+            parts,
+            feats,
+            other_feats,
+            round_up(used_rows, near_count * ROW_TILE),
+            middle not in slow,
         )
         head = summed(exchange(head.reshape(near_count, -1, LANES), near))
-        back = swap(sent, middle)
-        head = low(summed(gather(head, far, far_count)))
-        head = after(head, back)
-        txt = kept + wide(back)
-        back = swap(low(txt[:, 1]), top)
-        head = gather(head, near, near_count)
-        head = after(head, back)
-        txt = txt[:, 0] + wide(back)
         is_first = core_index == 0
-        own_txt = jnp.where(is_first, txt[0], txt[1])
-        back = swap(jnp.where(is_first, txt[1], txt[0]), core)
+        if middle in slow:
+            back = swap(sent, top)
+            head = after(head, back)
+            kept, sent = folded(kept, back)
+            back = swap(sent, middle)
+            head = low(summed(gather(head, far, far_count)))
+            head = gather(head, near, near_count)
+            own_txt, other_txt = finished(indices, kept, back)
+            head = after(head, other_txt)
+        else:
+            back = swap(sent, middle)
+            head = low(summed(gather(head, far, far_count)))
+            head = after(head, back)
+            txt = kept + wide(back)
+            back = swap(low(txt[:, 1]), top)
+            head = gather(head, near, near_count)
+            head = after(head, back)
+            txt = txt[:, 0] + wide(back)
+            own_txt = jnp.where(is_first, txt[0], txt[1])
+            other_txt = jnp.where(is_first, txt[1], txt[0])
+        back = swap(other_txt, core)
         text_grad = jnp.concatenate(
             [jnp.where(is_first, own_txt, back), jnp.where(is_first, back, own_txt)]
         ).T
@@ -221,7 +278,7 @@
         return head.reshape(share, width), text_grad
 
     def on_device(feats, weight, text, scale, bias, labels, plan):
-        middle_bit = jnp.max(jnp.where(plan == bits - 1, 0, plan))
+        middle_bit = plan[0] + plan[1] + plan[3] - (bits - 1)
         branches = [
             (lambda *args, name=f"b{bit}": with_middle(name, *args)) for bit in range(1, bits - 1)
         ]

time: 171 us -> 180 us (1.053)
  starting transfers between devices: 85 us -> 104 us
  waiting for transfers between devices: 43.7 us -> 26.7 us
  Pallas kernels: 7.01 us -> 10.6 us
  local copies, waits for them, and re-layouts: 2.61 us -> 5.44 us
    ppermute x8, waiting for transfers between devices: 24.8 us -> 8.48 us  [swap(): return lax.ppermute(shard, axis, SWAP)]
    ppermute x8, starting transfers between devices: 45 us -> 58.9 us  [swap(): return lax.ppermute(shard, axis, SWAP)]
    all_to_all x5, starting transfers between devices: 40 us -> 45 us  [exchange(): return lax.all_to_all(parts, axes, 0, 0, tiled=False)]
    pallas_call x1 -> x3, Pallas kernels: 1.73 us -> 5.31 us  [the longest x1 1.82 us: folded(): pl.pallas_call(fold_kernel, out_shape=(jax.ShapeDtypeStruct(shape, jnp.fl...]
  transfers between devices with their start and end apart: 13 -> 13, of which waited for: 9 -> 6; matrix products, arithmetic and copies ran while one was open for 2% -> 3% of each run, Pallas kernels for 2% -> 4%
where the time goes in v3:
time: 180 us; the launch traced here: 179 us
  starting transfers between devices  104 us (58%)
  waiting for transfers between devices  26.7 us (15%)
  blocking collectives  23.7 us (13%)
  Pallas kernels  10.6 us (6%)
  local copies, waits for them, and re-layouts  5.44 us (3%)
  other arithmetic  4.41 us (2%)
  between operations  2.51 us (1%)
    ppermute x8, starting transfers between devices, swap(): return lax.ppermute(shard, axis, SWAP)  58.9 us
    all_to_all x5, starting transfers between devices, exchange(): return lax.all_to_all(parts, axes, 0, 0, tiled=False)  45 us
    all_to_all x1, blocking collectives, exchange(): return lax.all_to_all(parts, axes, 0, 0, tiled=False)  23.7 us
    all_to_all x5, waiting for transfers between devices, exchange(): return lax.all_to_all(parts, axes, 0, 0, tiled=False)  18.2 us
    ppermute x8, waiting for transfers between devices, swap(): return lax.ppermute(shard, axis, SWAP)  8.48 us
    pallas_call x1, Pallas kernels, tile_parts(): pl.pallas_call(tile_kernel, out_shape=jax.ShapeDtypeStruct((2, parts, hal...  3.82 us
  transfers between devices with their start and end apart: 13, of which 6 were waited for; matrix products, arithmetic and copies ran while one was open for 3% of the time, Pallas kernels for 4%

profile of v3, /device:TPU:1, one launch (start us, length us, event | category | flops | bytes accessed | tf_op | source)
XLA Modules:
  0.0 179.3 jit_solution(418424182011336291)
XLA Ops:
  0.6 1.4 fusion.16
  3.9 175.4 %conditional.1 = (f32[144,1152]{1,0:T(8,128)}, f32[320,144]{0,1:T(8,128)}) conditional(s32[]{:T(128)} %bitcast.67, (f32[1]{0:T(128)}, f32[1]{0:T(128)}, bf16[144,1152]{1,0:T(8,128)(2,1)}, bf16[320,1152]{1,0:T(8,128)(2,1)}, bf16[320,144]{0,1:T(8,128)(2,1)}, /*index=5*/s32[1,320]{1,0:T(1,128)}) %tuple.47, (f32[1]{0:T(128)}, ...), branch_computations={%region_0.3_spmd, %region_3.6_spmd, %region_6.9_spmd, %region_9.12... | conditional | flops 100108451840 | bytes 132937896 | solution.py:285
  4.1 1.6 fusion.19
  5.7 0.1 pad_maximum_fusion.14
  5.8 1.2 broadcast_in_dim.33
  7.1 6.0 %all-to-all-start = ((f32[8,72,640]{2,1,0:T(8,128)}), f32[8,72,640]{2,1,0:T(8,128)S(1)}, u32[]{:S(2)}, u32[]{:S(2)}) async-start(f32[8,72,640]{2,1,0:T(8,128)} %broadcast_in_dim.33), calls=%async_computation | async-start | bytes 2949120 | tf_op jit(solution)/shard_map/cond/branch_2_fun/all_to_all | solution.py:25
  13.1 0.1 pad_maximum_fusion.16
  13.2 10.6 %collective-permute-start = (bf16[72,640]{1,0:T(8,128)(2,1)S(1)}, bf16[72,640]{1,0:T(8,128)(2,1)S(1)}, u32[]{:S(2)}, u32[]{:S(2)}) collective-permute-start(bf16[72,640]{1,0:T(8,128)(2,1)S(1)} %pad_maximum_fusion.16), channel_id=1, source_target_pairs={{0,64},{64,0},{1,65},{65,1},{2,66},{66,2},{3,67},{67,3},{4,68},{68... | collective-permute-start | bytes 276488 | tf_op jit(solution)/shard_map/cond/branch_2_fun/ppermute | solution.py:21
  23.8 0.1 fusion.34
  23.9 1.8 %collective-permute-done = bf16[72,640]{1,0:T(8,128)(2,1)S(1)} collective-permute-done((bf16[72,640]{1,0:T(8,128)(2,1)S(1)}, bf16[72,640]{1,0:T(8,128)(2,1)S(1)}, u32[]{:S(2)}, u32[]{:S(2)}) %collective-permute-start) | collective-permute-done | bytes 92192 | tf_op jit(solution)/shard_map/cond/branch_2_fun/ppermute | solution.py:21
  25.8 6.6 %collective-permute-start.1 = (bf16[2,72,640]{2,1,0:T(8,128)(2,1)S(1)}, bf16[2,72,640]{2,1,0:T(8,128)(2,1)S(1)}, u32[]{:S(2)}, u32[]{:S(2)}) collective-permute-start(bf16[2,72,640]{2,1,0:T(8,128)(2,1)S(1)} %pad_maximum_fusion.15), channel_id=1, source_target_pairs={{0,512},{512,0},{1,513},{513,1},{2,514},{514,2},{3,515},{515,3},{4... | collective-permute-start | bytes 552968 | tf_op jit(solution)/shard_map/cond/branch_2_fun/ppermute | solution.py:21
  32.3 5.3 %collective-permute-done.1 = bf16[2,72,640]{2,1,0:T(8,128)(2,1)S(1)} collective-permute-done((bf16[2,72,640]{2,1,0:T(8,128)(2,1)S(1)}, bf16[2,72,640]{2,1,0:T(8,128)(2,1)S(1)}, u32[]{:S(2)}, u32[]{:S(2)}) %collective-permute-start.1) | collective-permute-done | bytes 184352 | tf_op jit(solution)/shard_map/cond/branch_2_fun/ppermute | solution.py:21
  37.7 0.0 copy-start.20
  37.7 13.0 %collective-permute-start.2 = (bf16[4,72,640]{2,1,0:T(8,128)(2,1)S(1)}, bf16[4,72,640]{2,1,0:T(8,128)(2,1)S(1)}, u32[]{:S(2)}, u32[]{:S(2)}) collective-permute-start(bf16[4,72,640]{2,1,0:T(8,128)(2,1)S(1)} %pad_maximum_fusion.13), channel_id=1, source_target_pairs={{0,8},{8,0},{1,9},{9,1},{2,10},{10,2},{3,11},{11,3},{4,12},{12,4},... | collective-permute-start | bytes 1105928 | tf_op jit(solution)/shard_map/cond/branch_2_fun/ppermute | solution.py:21
  50.7 1.3 collective-permute-done.2
  52.0 1.0 pad_maximum_fusion.12
  53.0 5.3 %all-to-all-start.1 = ((bf16[8,72,640]{2,1,0:T(8,128)(2,1)}), bf16[8,72,640]{2,1,0:T(8,128)(2,1)S(1)}, u32[]{:S(2)}, u32[]{:S(2)}) async-start(bf16[8,72,640]{2,1,0:T(8,128)(2,1)} %pad_maximum_fusion.12), calls=%async_computation.1 | async-start | bytes 1474560 | tf_op jit(solution)/shard_map/cond/branch_2_fun/all_to_all | solution.py:25
  58.3 2.6 %collective-permute-start.3 = (bf16[320,1152]{1,0:T(8,128)(2,1)}, bf16[320,1152]{1,0:T(8,128)(2,1)S(1)}, u32[]{:S(2)}, u32[]{:S(2)}) collective-permute-start(bf16[320,1152]{1,0:T(8,128)(2,1)} %get-tuple-element.90.feats_ref), channel_id=1, source_target_pairs={{0,8},{8,0},{1,9},{9,1},{2,10},{10,2},{3,11},{11,3},{4,12},{12,4},... | collective-permute-start | bytes 2211848 | tf_op jit(solution)/shard_map/cond/branch_2_fun/ppermute | solution.py:21
  60.9 0.1 pad_add_fusion.2.index_ref
  61.0 1.4 pad_maximum_fusion.17.number_ref
  62.3 7.5 %all-to-all-done.1.text_ref = bf16[8,72,640]{2,1,0:T(8,128)(2,1)S(1)} async-done(((bf16[8,72,640]{2,1,0:T(8,128)(2,1)}), bf16[8,72,640]{2,1,0:T(8,128)(2,1)S(1)}, u32[]{:S(2)}, u32[]{:S(2)}) %all-to-all-start.1) | async-done | bytes 737312 | tf_op jit(solution)/shard_map/cond/branch_2_fun/all_to_all | solution.py:25
  69.8 3.8 %tile_parts.7 = bf16[2,8,72,640]{3,2,1,0:T(8,128)(2,1)S(1)} custom-call(f32[2]{0:T(128)S(1)} %pad_maximum_fusion.17.number_ref, s32[2]{0:T(128)S(1)} %pad_add_fusion.2.index_ref, s32[1,320]{1,0:T(1,128)S(1)} %copy-done.20, f32[8,72,640]{2,1,0:T(8,128)S(1)} %all-to-all-done.embed_ref, bf16[8,72,640]{2,1,0:T(8,128)(2,1)S(1)} %all-to-all-done.1.text_ref), custom_call_target="tpu_custom_call" | custom-call | tf_op jit(solution)/shard_map/cond/branch_2_fun/tile_parts/pallas_call | solution.py:96
  73.7 0.0 copy-start.8
  73.7 23.7 %all_to_all.122 = bf16[16,72,640]{2,1,0:T(8,128)(2,1)S(1)} all-to-all(bf16[16,72,640]{2,1,0:T(8,128)(2,1)S(1)} %bitcast.111), channel_id=1, replica_groups=mesh['b6'=2,'b5'=2,'b4'=2,'b3'=2,'b2'=2,'b1'=2,'b0'=2,'x'=4,'y'=2] {'b0'..., dimensions={0} | all-to-all | bytes 2949120 | tf_op jit(solution)/shard_map/cond/branch_2_fun/all_to_all | solution.py:25
  97.4 1.7 head_rows.7
  99.2 0.8 copy-done
  99.9 13.5 %all-to-all-start.3 = ((bf16[16,48,128]{2,1,0:T(8,128)(2,1)}), bf16[16,48,128]{2,1,0:T(8,128)(2,1)S(1)}, u32[]{:S(2)}, u32[]{:S(2)}) async-start(bf16[16,48,128]{2,1,0:T(8,128)(2,1)} %bitcast.37), calls=%async_computation.3 | async-start | bytes 393216 | tf_op jit(solution)/shard_map/cond/branch_2_fun/all_to_all | solution.py:25
  113.4 6.7 %collective-permute-start.4 = (bf16[2,2,72,320]{3,2,1,0:T(8,128)(2,1)S(1)}, bf16[2,2,72,320]{3,2,1,0:T(8,128)(2,1)S(1)}, u32[]{:S(2)}, u32[]{:S(2)}) collective-permute-start(bf16[2,2,72,320]{3,2,1,0:T(8,128)(2,1)S(1)} %get-tuple-element.95), channel_id=1, source_target_pairs={{0,512},{512,0},{1,513},{513,1},{2,514},{514,2},{3,515},{515,3},{4... | collective-permute-start | bytes 552968 | tf_op jit(solution)/shard_map/cond/branch_2_fun/ppermute | solution.py:21
  120.1 5.6 %all-to-all-done.3 = bf16[16,48,128]{2,1,0:T(8,128)(2,1)S(1)} async-done(((bf16[16,48,128]{2,1,0:T(8,128)(2,1)}), bf16[16,48,128]{2,1,0:T(8,128)(2,1)S(1)}, u32[]{:S(2)}, u32[]{:S(2)}) %all-to-all-start.3) | async-done | bytes 196640 | tf_op jit(solution)/shard_map/cond/branch_2_fun/all_to_all | solution.py:25
  125.8 0.0 collective-permute-done.4.back_ref
  125.8 0.0 copy-start.16
  125.8 0.7 broadcast_in_dim.34
  126.5 10.6 %all-to-all-start.4 = ((f32[4,48,128]{2,1,0:T(8,128)}), f32[4,48,128]{2,1,0:T(8,128)S(1)}, u32[]{:S(2)}, u32[]{:S(2)}) async-start(f32[4,48,128]{2,1,0:T(8,128)} %broadcast_in_dim.34), calls=%async_computation.4 | async-start | bytes 196608 | tf_op jit(solution)/shard_map/cond/branch_2_fun/all_to_all | solution.py:25
  137.1 1.8 %folded.2 = (f32[2,72,320]{2,1,0:T(8,128)}, bf16[2,72,320]{2,1,0:T(8,128)(2,1)}) custom-call(f32[2,2,72,320]{3,2,1,0:T(8,128)} %copy-done, bf16[2,2,72,320]{3,2,1,0:T(8,128)(2,1)} %copy-done.16), custom_call_target="tpu_custom_call" | custom-call | tf_op jit(solution)/shard_map/cond/branch_2_fun/folded/pallas_call | solution.py:154
  138.9 7.2 %collective-permute-start.5 = (bf16[2,72,320]{2,1,0:T(8,128)(2,1)}, bf16[2,72,320]{2,1,0:T(8,128)(2,1)S(1)}, u32[]{:S(2)}, u32[]{:S(2)}) collective-permute-start(bf16[2,72,320]{2,1,0:T(8,128)(2,1)} %get-tuple-element.99), channel_id=1, source_target_pairs={{0,64},{64,0},{1,65},{65,1},{2,66},{66,2},{3,67},{67,3},{4,68},{68... | collective-permute-start | bytes 276488 | tf_op jit(solution)/shard_map/cond/branch_2_fun/ppermute | solution.py:21
  146.1 0.7 broadcast_in_dim.35
  146.8 9.6 %all-to-all-start.5 = ((bf16[16,48,128]{2,1,0:T(8,128)(2,1)}), bf16[16,48,128]{2,1,0:T(8,128)(2,1)S(1)}, u32[]{:S(2)}, u32[]{:S(2)}) async-start(bf16[16,48,128]{2,1,0:T(8,128)(2,1)} %broadcast_in_dim.35), calls=%async_computation.5 | async-start | bytes 393216 | tf_op jit(solution)/shard_map/cond/branch_2_fun/all_to_all | solution.py:25
  156.4 0.0 collective-permute-done.5.back_ref
  156.4 0.0 copy-start.23
  156.4 0.6 copy-done.23
  157.1 1.7 finished.2
  158.8 4.8 %collective-permute-start.7 = (f32[72,320]{1,0:T(8,128)}, f32[72,320]{1,0:T(8,128)S(1)}, u32[]{:S(2)}, u32[]{:S(2)}) collective-permute-start(f32[72,320]{1,0:T(8,128)} %get-tuple-element.100), channel_id=1, source_target_pairs={{0,8},{8,0},{1,9},{9,1},{2,10},{10,2},{3,11},{11,3},{4,12},{12,4},... | collective-permute-start | bytes 276488 | tf_op jit(solution)/shard_map/cond/branch_2_fun/ppermute | solution.py:21
  163.6 5.1 %all-to-all-done.5 = bf16[16,48,128]{2,1,0:T(8,128)(2,1)S(1)} async-done(((bf16[16,48,128]{2,1,0:T(8,128)(2,1)}), bf16[16,48,128]{2,1,0:T(8,128)(2,1)S(1)}, u32[]{:S(2)}, u32[]{:S(2)}) %all-to-all-start.5) | async-done | bytes 196640 | tf_op jit(solution)/shard_map/cond/branch_2_fun/all_to_all | solution.py:25
  168.8 7.5 %collective-permute-start.6 = (bf16[768,128]{1,0:T(8,128)(2,1)S(1)}, bf16[768,128]{1,0:T(8,128)(2,1)S(1)}, u32[]{:S(2)}, u32[]{:S(2)}) collective-permute-start(bf16[768,128]{1,0:T(8,128)(2,1)S(1)} %bitcast.125), channel_id=1, source_target_pairs={{0,8},{8,0},{1,9},{9,1},{2,10},{10,2},{3,11},{11,3},{4,12},{12,4},... | collective-permute-start | bytes 589832 | tf_op jit(solution)/shard_map/cond/branch_2_fun/ppermute | solution.py:21
  176.2 0.0 collective-permute-done.7
  176.2 0.9 broadcast_select_fusion.1
  177.2 0.7 maximum_bitcast_fusion.2
  177.9 1.4 unpacked.7
  (20 shorter events, 0.2 us)
Async XLA Ops:
  7.1 6.0 %copy-start.13 = (bf16[320,144]{0,1:T(8,128)(2,1)S(1)}, bf16[320,144]{0,1:T(8,128)(2,1)}, u32[]{:S(2)}) copy-start(bf16[320,144]{0,1:T(8,128)(2,1)} %get-tuple-element.91) | copy-start | bytes 276484 | tf_op jit(solution)/shard_map/cond
  7.1 45.9 %all-to-all-start = ((f32[8,72,640]{2,1,0:T(8,128)}), f32[8,72,640]{2,1,0:T(8,128)S(1)}, u32[]{:S(2)}, u32[]{:S(2)}) async-start(f32[8,72,640]{2,1,0:T(8,128)} %broadcast_in_dim.33), calls=%async_computation | async-start | bytes 2949120 | tf_op jit(solution)/shard_map/cond/branch_2_fun/all_to_all | solution.py:25
  13.2 12.6 %collective-permute-start = (bf16[72,640]{1,0:T(8,128)(2,1)S(1)}, bf16[72,640]{1,0:T(8,128)(2,1)S(1)}, u32[]{:S(2)}, u32[]{:S(2)}) collective-permute-start(bf16[72,640]{1,0:T(8,128)(2,1)S(1)} %pad_maximum_fusion.16), channel_id=1, source_target_pairs={{0,64},{64,0},{1,65},{65,1},{2,66},{66,2},{3,67},{67,3},{4,68},{68... | collective-permute-start | bytes 276488 | tf_op jit(solution)/shard_map/cond/branch_2_fun/ppermute | solution.py:21
  25.8 11.9 %collective-permute-start.1 = (bf16[2,72,640]{2,1,0:T(8,128)(2,1)S(1)}, bf16[2,72,640]{2,1,0:T(8,128)(2,1)S(1)}, u32[]{:S(2)}, u32[]{:S(2)}) collective-permute-start(bf16[2,72,640]{2,1,0:T(8,128)(2,1)S(1)} %pad_maximum_fusion.15), channel_id=1, source_target_pairs={{0,512},{512,0},{1,513},{513,1},{2,514},{514,2},{3,515},{515,3},{4... | collective-permute-start | bytes 552968 | tf_op jit(solution)/shard_map/cond/branch_2_fun/ppermute | solution.py:21
  37.7 32.1 %copy-start.20 = (s32[1,320]{1,0:T(1,128)S(1)}, s32[1,320]{1,0:T(1,128)}, u32[]{:S(2)}) copy-start(s32[1,320]{1,0:T(1,128)} %get-tuple-element.88.label_ref) | copy-start | bytes 3844 | tf_op jit(solution)/shard_map/cond
  37.7 14.3 %collective-permute-start.2 = (bf16[4,72,640]{2,1,0:T(8,128)(2,1)S(1)}, bf16[4,72,640]{2,1,0:T(8,128)(2,1)S(1)}, u32[]{:S(2)}, u32[]{:S(2)}) collective-permute-start(bf16[4,72,640]{2,1,0:T(8,128)(2,1)S(1)} %pad_maximum_fusion.13), channel_id=1, source_target_pairs={{0,8},{8,0},{1,9},{9,1},{2,10},{10,2},{3,11},{11,3},{4,12},{12,4},... | collective-permute-start | bytes 1105928 | tf_op jit(solution)/shard_map/cond/branch_2_fun/ppermute | solution.py:21
  53.0 16.8 %all-to-all-start.1 = ((bf16[8,72,640]{2,1,0:T(8,128)(2,1)}), bf16[8,72,640]{2,1,0:T(8,128)(2,1)S(1)}, u32[]{:S(2)}, u32[]{:S(2)}) async-start(bf16[8,72,640]{2,1,0:T(8,128)(2,1)} %pad_maximum_fusion.12), calls=%async_computation.1 | async-start | bytes 1474560 | tf_op jit(solution)/shard_map/cond/branch_2_fun/all_to_all | solution.py:25
  58.3 15.3 %collective-permute-start.3 = (bf16[320,1152]{1,0:T(8,128)(2,1)}, bf16[320,1152]{1,0:T(8,128)(2,1)S(1)}, u32[]{:S(2)}, u32[]{:S(2)}) collective-permute-start(bf16[320,1152]{1,0:T(8,128)(2,1)} %get-tuple-element.90.feats_ref), channel_id=1, source_target_pairs={{0,8},{8,0},{1,9},{9,1},{2,10},{10,2},{3,11},{11,3},{4,12},{12,4},... | collective-permute-start | bytes 2211848 | tf_op jit(solution)/shard_map/cond/branch_2_fun/ppermute | solution.py:21
  61.0 36.4 %copy-start.2 = (s32[2]{0:T(128)}, s32[2]{0:T(128)S(1)}, u32[]{:S(2)}) copy-start(s32[2]{0:T(128)S(1)} %pad_add_fusion.2.index_ref) | copy-start | bytes 28 | tf_op jit(solution)/shard_map/cond
  73.7 23.8 %copy-start.8 = (bf16[320,1152]{1,0:T(8,128)(2,1)S(1)}, bf16[320,1152]{1,0:T(8,128)(2,1)}, u32[]{:S(2)}) copy-start(bf16[320,1152]{1,0:T(8,128)(2,1)} %get-tuple-element.90.feats_ref) | copy-start | bytes 2211844 | tf_op jit(solution)/shard_map/cond
  99.2 0.8 copy-start
  99.9 25.8 %all-to-all-start.3 = ((bf16[16,48,128]{2,1,0:T(8,128)(2,1)}), bf16[16,48,128]{2,1,0:T(8,128)(2,1)S(1)}, u32[]{:S(2)}, u32[]{:S(2)}) async-start(bf16[16,48,128]{2,1,0:T(8,128)(2,1)} %bitcast.37), calls=%async_computation.3 | async-start | bytes 393216 | tf_op jit(solution)/shard_map/cond/branch_2_fun/all_to_all | solution.py:25
  113.4 12.4 %collective-permute-start.4 = (bf16[2,2,72,320]{3,2,1,0:T(8,128)(2,1)S(1)}, bf16[2,2,72,320]{3,2,1,0:T(8,128)(2,1)S(1)}, u32[]{:S(2)}, u32[]{:S(2)}) collective-permute-start(bf16[2,2,72,320]{3,2,1,0:T(8,128)(2,1)S(1)} %get-tuple-element.95), channel_id=1, source_target_pairs={{0,512},{512,0},{1,513},{513,1},{2,514},{514,2},{3,515},{515,3},{4... | collective-permute-start | bytes 552968 | tf_op jit(solution)/shard_map/cond/branch_2_fun/ppermute | solution.py:21
  125.8 11.3 %copy-start.16 = (bf16[2,2,72,320]{3,2,1,0:T(8,128)(2,1)}, bf16[2,2,72,320]{3,2,1,0:T(8,128)(2,1)S(1)}, u32[]{:S(2)}) copy-start(bf16[2,2,72,320]{3,2,1,0:T(8,128)(2,1)S(1)} %collective-permute-done.4.back_ref) | copy-start | bytes 552964 | tf_op jit(solution)/shard_map/cond
  126.5 19.6 %all-to-all-start.4 = ((f32[4,48,128]{2,1,0:T(8,128)}), f32[4,48,128]{2,1,0:T(8,128)S(1)}, u32[]{:S(2)}, u32[]{:S(2)}) async-start(f32[4,48,128]{2,1,0:T(8,128)} %broadcast_in_dim.34), calls=%async_computation.4 | async-start | bytes 196608 | tf_op jit(solution)/shard_map/cond/branch_2_fun/all_to_all | solution.py:25
  138.9 17.5 %collective-permute-start.5 = (bf16[2,72,320]{2,1,0:T(8,128)(2,1)}, bf16[2,72,320]{2,1,0:T(8,128)(2,1)S(1)}, u32[]{:S(2)}, u32[]{:S(2)}) collective-permute-start(bf16[2,72,320]{2,1,0:T(8,128)(2,1)} %get-tuple-element.99), channel_id=1, source_target_pairs={{0,64},{64,0},{1,65},{65,1},{2,66},{66,2},{3,67},{67,3},{4,68},{68... | collective-permute-start | bytes 276488 | tf_op jit(solution)/shard_map/cond/branch_2_fun/ppermute | solution.py:21
  146.8 22.0 %all-to-all-start.5 = ((bf16[16,48,128]{2,1,0:T(8,128)(2,1)}), bf16[16,48,128]{2,1,0:T(8,128)(2,1)S(1)}, u32[]{:S(2)}, u32[]{:S(2)}) async-start(bf16[16,48,128]{2,1,0:T(8,128)(2,1)} %broadcast_in_dim.35), calls=%async_computation.5 | async-start | bytes 393216 | tf_op jit(solution)/shard_map/cond/branch_2_fun/all_to_all | solution.py:25
  156.4 0.6 copy-start.23
  157.1 20.8 %copy-start.3 = (s32[2]{0:T(128)S(1)}, s32[2]{0:T(128)}, u32[]{:S(2)}) copy-start(s32[2]{0:T(128)} %copy-done.2) | copy-start | bytes 28 | tf_op jit(solution)/shard_map/cond
  158.8 17.4 %collective-permute-start.7 = (f32[72,320]{1,0:T(8,128)}, f32[72,320]{1,0:T(8,128)S(1)}, u32[]{:S(2)}, u32[]{:S(2)}) collective-permute-start(f32[72,320]{1,0:T(8,128)} %get-tuple-element.100), channel_id=1, source_target_pairs={{0,8},{8,0},{1,9},{9,1},{2,10},{10,2},{3,11},{11,3},{4,12},{12,4},... | collective-permute-start | bytes 276488 | tf_op jit(solution)/shard_map/cond/branch_2_fun/ppermute | solution.py:21
  168.8 9.1 %collective-permute-start.6 = (bf16[768,128]{1,0:T(8,128)(2,1)S(1)}, bf16[768,128]{1,0:T(8,128)(2,1)S(1)}, u32[]{:S(2)}, u32[]{:S(2)}) collective-permute-start(bf16[768,128]{1,0:T(8,128)(2,1)S(1)} %bitcast.125), channel_id=1, source_target_pairs={{0,8},{8,0},{1,9},{9,1},{2,10},{10,2},{3,11},{11,3},{4,12},{12,4},... | collective-permute-start | bytes 589832 | tf_op jit(solution)/shard_map/cond/branch_2_fun/ppermute | solution.py:21

commit v4 on v3

--- a/solution.py
+++ b/solution.py
@@ -278,7 +278,7 @@
         return head.reshape(share, width), text_grad
 
     def on_device(feats, weight, text, scale, bias, labels, plan):
-        middle_bit = plan[0] + plan[1] + plan[3] - (bits - 1)
+        middle_bit = jnp.max(jnp.where(plan == bits - 1, 0, plan))
         branches = [
             (lambda *args, name=f"b{bit}": with_middle(name, *args)) for bit in range(1, bits - 1)
         ]

time: 180 us -> 166 us (0.922)
  starting transfers between devices: 104 us -> 78.3 us
  waiting for transfers between devices: 26.7 us -> 45.7 us
  Pallas kernels: 10.6 us -> 7.03 us
  local copies, waits for them, and re-layouts: 5.44 us -> 2.63 us
    ppermute x8, starting transfers between devices: 58.9 us -> 38.4 us  [swap(): return lax.ppermute(shard, axis, SWAP)]
    ppermute x8, waiting for transfers between devices: 8.48 us -> 21.9 us  [swap(): return lax.ppermute(shard, axis, SWAP)]
    all_to_all x5, waiting for transfers between devices: 18.2 us -> 23.8 us  [exchange(): return lax.all_to_all(parts, axes, 0, 0, tiled=False)]
    all_to_all x5, starting transfers between devices: 45 us -> 39.9 us  [exchange(): return lax.all_to_all(parts, axes, 0, 0, tiled=False)]
    pallas_call x2 -> x0, Pallas kernels: 3.56 us -> none  [the longest x1 1.82 us: folded(): pl.pallas_call(fold_kernel, out_shape=(jax.ShapeDtypeStruct(shape, jnp.fl...]
  transfers between devices with their start and end apart: 13 -> 13, of which waited for: 6 -> 8; matrix products, arithmetic and copies ran while one was open for 3% -> 3% of each run, Pallas kernels for 4% -> 2%
where the time goes in v4:
time: 166 us; the launch traced here: 165 us
  starting transfers between devices  78.3 us (47%)
  waiting for transfers between devices  45.7 us (28%)
  blocking collectives  23.7 us (14%)
  Pallas kernels  7.03 us (4%)
  other arithmetic  4.87 us (3%)
  local copies, waits for them, and re-layouts  2.63 us (2%)
    all_to_all x5, starting transfers between devices, exchange(): return lax.all_to_all(parts, axes, 0, 0, tiled=False)  39.9 us
    ppermute x8, starting transfers between devices, swap(): return lax.ppermute(shard, axis, SWAP)  38.4 us
    all_to_all x5, waiting for transfers between devices, exchange(): return lax.all_to_all(parts, axes, 0, 0, tiled=False)  23.8 us
    all_to_all x1, blocking collectives, exchange(): return lax.all_to_all(parts, axes, 0, 0, tiled=False)  23.7 us
    ppermute x8, waiting for transfers between devices, swap(): return lax.ppermute(shard, axis, SWAP)  21.9 us
    pallas_call x1, Pallas kernels, tile_parts(): pl.pallas_call(tile_kernel, out_shape=jax.ShapeDtypeStruct((2, parts, hal...  3.86 us
  transfers between devices with their start and end apart: 13, of which 8 were waited for; matrix products, arithmetic and copies ran while one was open for 3% of the time, Pallas kernels for 2%

profile of v4, /device:TPU:1, one launch (start us, length us, event | category | flops | bytes accessed | tf_op | source)
XLA Modules:
  0.0 165.5 jit_solution(5080323281124263550)
XLA Ops:
  0.6 1.3 fusion.6
  2.6 162.9 %conditional.1 = (f32[144,1152]{1,0:T(8,128)}, f32[320,144]{0,1:T(8,128)}) conditional(s32[]{:T(128)} %clamp.3, (f32[1]{0:T(128)}, f32[1]{0:T(128)}, bf16[144,1152]{1,0:T(8,128)(2,1)}, bf16[320,1152]{1,0:T(8,128)(2,1)}, bf16[320,144]{0,1:T(8,128)(2,1)}, /*index=5*/s32[1,320]{1,0:T(1,128)}) %tuple.47, (f32[1]{0:T(128)}, ...), branch_computations={%region_1.4_spmd, %region_4.7_spmd, %region_7.10_spmd, %region_10.... | conditional | flops 100108451840 | bytes 132937896 | solution.py:285
  2.6 1.6 fusion.17
  4.3 0.1 pad_maximum_fusion.2
  4.4 1.2 broadcast_in_dim.26
  5.6 6.0 %all-to-all-start.12 = ((f32[8,72,640]{2,1,0:T(8,128)}), f32[8,72,640]{2,1,0:T(8,128)S(1)}, u32[]{:S(2)}, u32[]{:S(2)}) async-start(f32[8,72,640]{2,1,0:T(8,128)} %broadcast_in_dim.26), calls=%async_computation.12 | async-start | bytes 2949120 | tf_op jit(solution)/shard_map/cond/branch_0_fun/all_to_all | solution.py:25
  11.6 0.0 copy-done.11
  11.6 0.1 pad_maximum_fusion.4
  11.7 4.0 %collective-permute-start.16 = (bf16[72,640]{1,0:T(8,128)(2,1)S(1)}, bf16[72,640]{1,0:T(8,128)(2,1)S(1)}, u32[]{:S(2)}, u32[]{:S(2)}) collective-permute-start(bf16[72,640]{1,0:T(8,128)(2,1)S(1)} %pad_maximum_fusion.4), channel_id=1, source_target_pairs={{0,16},{16,0},{1,17},{17,1},{2,18},{18,2},{3,19},{19,3},{4,20},{20... | collective-permute-start | bytes 276488 | tf_op jit(solution)/shard_map/cond/branch_0_fun/ppermute | solution.py:21
  15.7 0.1 fusion.32
  15.8 1.8 %collective-permute-done.16 = bf16[72,640]{1,0:T(8,128)(2,1)S(1)} collective-permute-done((bf16[72,640]{1,0:T(8,128)(2,1)S(1)}, bf16[72,640]{1,0:T(8,128)(2,1)S(1)}, u32[]{:S(2)}, u32[]{:S(2)}) %collective-permute-start.16) | collective-permute-done | bytes 92192 | tf_op jit(solution)/shard_map/cond/branch_0_fun/ppermute | solution.py:21
  17.7 6.8 %collective-permute-start.17 = (bf16[2,72,640]{2,1,0:T(8,128)(2,1)S(1)}, bf16[2,72,640]{2,1,0:T(8,128)(2,1)S(1)}, u32[]{:S(2)}, u32[]{:S(2)}) collective-permute-start(bf16[2,72,640]{2,1,0:T(8,128)(2,1)S(1)} %pad_maximum_fusion.3), channel_id=1, source_target_pairs={{0,512},{512,0},{1,513},{513,1},{2,514},{514,2},{3,515},{515,3},{4... | collective-permute-start | bytes 552968 | tf_op jit(solution)/shard_map/cond/branch_0_fun/ppermute | solution.py:21
  24.5 11.2 %collective-permute-done.17 = bf16[2,72,640]{2,1,0:T(8,128)(2,1)S(1)} collective-permute-done((bf16[2,72,640]{2,1,0:T(8,128)(2,1)S(1)}, bf16[2,72,640]{2,1,0:T(8,128)(2,1)S(1)}, u32[]{:S(2)}, u32[]{:S(2)}) %collective-permute-start.17) | collective-permute-done | bytes 184352 | tf_op jit(solution)/shard_map/cond/branch_0_fun/ppermute | solution.py:21
  35.8 0.0 copy-start.18
  35.8 8.7 %collective-permute-start.18 = (bf16[4,72,640]{2,1,0:T(8,128)(2,1)S(1)}, bf16[4,72,640]{2,1,0:T(8,128)(2,1)S(1)}, u32[]{:S(2)}, u32[]{:S(2)}) collective-permute-start(bf16[4,72,640]{2,1,0:T(8,128)(2,1)S(1)} %pad_maximum_fusion.1), channel_id=1, source_target_pairs={{0,8},{8,0},{1,9},{9,1},{2,10},{10,2},{3,11},{11,3},{4,12},{12,4},... | collective-permute-start | bytes 1105928 | tf_op jit(solution)/shard_map/cond/branch_0_fun/ppermute | solution.py:21
  44.5 1.3 collective-permute-done.18
  45.8 1.0 pad_maximum_fusion
  46.8 0.0 all-to-all-done.12.embed_ref
  46.8 5.0 %all-to-all-start.13 = ((bf16[8,72,640]{2,1,0:T(8,128)(2,1)}), bf16[8,72,640]{2,1,0:T(8,128)(2,1)S(1)}, u32[]{:S(2)}, u32[]{:S(2)}) async-start(bf16[8,72,640]{2,1,0:T(8,128)(2,1)} %pad_maximum_fusion), calls=%async_computation.13 | async-start | bytes 1474560 | tf_op jit(solution)/shard_map/cond/branch_0_fun/all_to_all | solution.py:25
  51.7 2.6 %collective-permute-start.19 = (bf16[320,1152]{1,0:T(8,128)(2,1)}, bf16[320,1152]{1,0:T(8,128)(2,1)S(1)}, u32[]{:S(2)}, u32[]{:S(2)}) collective-permute-start(bf16[320,1152]{1,0:T(8,128)(2,1)} %get-tuple-element.64.feats_ref), channel_id=1, source_target_pairs={{0,8},{8,0},{1,9},{9,1},{2,10},{10,2},{3,11},{11,3},{4,12},{12,4},... | collective-permute-start | bytes 2211848 | tf_op jit(solution)/shard_map/cond/branch_0_fun/ppermute | solution.py:21
  54.3 0.1 pad_add_fusion.index_ref
  54.4 1.4 pad_maximum_fusion.5.number_ref
  55.7 7.5 %all-to-all-done.13.text_ref = bf16[8,72,640]{2,1,0:T(8,128)(2,1)S(1)} async-done(((bf16[8,72,640]{2,1,0:T(8,128)(2,1)}), bf16[8,72,640]{2,1,0:T(8,128)(2,1)S(1)}, u32[]{:S(2)}, u32[]{:S(2)}) %all-to-all-start.13) | async-done | bytes 737312 | tf_op jit(solution)/shard_map/cond/branch_0_fun/all_to_all | solution.py:25
  63.2 0.0 copy-done.18
  63.2 3.9 %tile_parts.5 = bf16[2,8,72,640]{3,2,1,0:T(8,128)(2,1)S(1)} custom-call(f32[2]{0:T(128)S(1)} %pad_maximum_fusion.5.number_ref, s32[2]{0:T(128)S(1)} %pad_add_fusion.index_ref, s32[1,320]{1,0:T(1,128)S(1)} %copy-done.18, f32[8,72,640]{2,1,0:T(8,128)S(1)} %all-to-all-done.12.embed_ref, bf16[8,72,640]{2,1,0:T(8,128)(2,1)S(1)} %all-to-all-done.13.text_ref), custom_call_target="tpu_custom_call" | custom-call | tf_op jit(solution)/shard_map/cond/branch_0_fun/tile_parts/pallas_call | solution.py:96
  67.1 0.0 collective-permute-done.19.other_ref
  67.1 0.0 copy-start.6
  67.1 23.7 %all_to_all.120 = bf16[16,72,640]{2,1,0:T(8,128)(2,1)S(1)} all-to-all(bf16[16,72,640]{2,1,0:T(8,128)(2,1)S(1)} %bitcast.108), channel_id=1, replica_groups=mesh['b6'=2,'b5'=2,'b4'=2,'b3'=2,'b2'=2,'b1'=2,'b0'=2,'x'=4,'y'=2] {'b0'..., dimensions={0} | all-to-all | bytes 2949120 | tf_op jit(solution)/shard_map/cond/branch_0_fun/all_to_all | solution.py:25
  90.8 0.0 copy-done.6
  90.8 1.7 %head_rows.5 = (bf16[768,128]{1,0:T(8,128)(2,1)}, f32[2,2,72,320]{3,2,1,0:T(8,128)S(1)}, bf16[2,2,72,320]{3,2,1,0:T(8,128)(2,1)S(1)}) custom-call(s32[2]{0:T(128)S(1)} %pad_add_fusion.index_ref, bf16[2,8,72,640]{3,2,1,0:T(8,128)(2,1)S(1)} %bitcast.113, bf16[320,1152]{1,0:T(8,128)(2,1)S(1)} %copy-done.6, bf16[320,1152]{1,0:T(8,128)(2,1)S(1)} %collective-permute-done.19.other_ref), custom_call_target="tpu_custom_call" | custom-call | tf_op jit(solution)/shard_map/cond/branch_0_fun/head_rows/pallas_call | solution.py:133
  92.6 18.4 %all-to-all-start.15 = ((bf16[16,48,128]{2,1,0:T(8,128)(2,1)}), bf16[16,48,128]{2,1,0:T(8,128)(2,1)S(1)}, u32[]{:S(2)}, u32[]{:S(2)}) async-start(bf16[16,48,128]{2,1,0:T(8,128)(2,1)} %bitcast.7), calls=%async_computation.15 | async-start | bytes 393216 | tf_op jit(solution)/shard_map/cond/branch_0_fun/all_to_all | solution.py:25
  110.9 3.3 %collective-permute-start.20 = (bf16[2,2,72,320]{3,2,1,0:T(8,128)(2,1)S(1)}, bf16[2,2,72,320]{3,2,1,0:T(8,128)(2,1)S(1)}, u32[]{:S(2)}, u32[]{:S(2)}) collective-permute-start(bf16[2,2,72,320]{3,2,1,0:T(8,128)(2,1)S(1)} %get-tuple-element.69), channel_id=1, source_target_pairs={{0,16},{16,0},{1,17},{17,1},{2,18},{18,2},{3,19},{19,3},{4,20},{20... | collective-permute-start | bytes 552968 | tf_op jit(solution)/shard_map/cond/branch_0_fun/ppermute | solution.py:21
  114.2 9.1 %all-to-all-done.15 = bf16[16,48,128]{2,1,0:T(8,128)(2,1)S(1)} async-done(((bf16[16,48,128]{2,1,0:T(8,128)(2,1)}), bf16[16,48,128]{2,1,0:T(8,128)(2,1)S(1)}, u32[]{:S(2)}, u32[]{:S(2)}) %all-to-all-start.15) | async-done | bytes 196640 | tf_op jit(solution)/shard_map/cond/branch_0_fun/all_to_all | solution.py:25
  123.3 0.6 broadcast_in_dim.27
  124.0 3.3 %all-to-all-start.16 = ((f32[4,48,128]{2,1,0:T(8,128)}), f32[4,48,128]{2,1,0:T(8,128)S(1)}, u32[]{:S(2)}, u32[]{:S(2)}) async-start(f32[4,48,128]{2,1,0:T(8,128)} %broadcast_in_dim.27), calls=%async_computation.16 | async-start | bytes 196608 | tf_op jit(solution)/shard_map/cond/branch_0_fun/all_to_all | solution.py:25
  127.3 0.0 collective-permute-done.20
  127.3 7.2 %all-to-all-done.16 = f32[4,48,128]{2,1,0:T(8,128)S(1)} async-done(((f32[4,48,128]{2,1,0:T(8,128)}), f32[4,48,128]{2,1,0:T(8,128)S(1)}, u32[]{:S(2)}, u32[]{:S(2)}) %all-to-all-start.16) | async-done | bytes 98336 | tf_op jit(solution)/shard_map/cond/branch_0_fun/all_to_all | solution.py:25
  134.5 0.7 broadcast_in_dim.32
  135.3 7.3 %all-to-all-start.17 = ((bf16[16,48,128]{2,1,0:T(8,128)(2,1)}), bf16[16,48,128]{2,1,0:T(8,128)(2,1)S(1)}, u32[]{:S(2)}, u32[]{:S(2)}) async-start(bf16[16,48,128]{2,1,0:T(8,128)(2,1)} %broadcast_in_dim.32), calls=%async_computation.17 | async-start | bytes 393216 | tf_op jit(solution)/shard_map/cond/branch_0_fun/all_to_all | solution.py:25
  142.6 2.2 %collective-permute-start.21 = (bf16[2,72,320]{2,1,0:T(8,128)(2,1)S(1)}, bf16[2,72,320]{2,1,0:T(8,128)(2,1)S(1)}, u32[]{:S(2)}, u32[]{:S(2)}) collective-permute-start(bf16[2,72,320]{2,1,0:T(8,128)(2,1)S(1)} %fusion.1), channel_id=1, source_target_pairs={{0,512},{512,0},{1,513},{513,1},{2,514},{514,2},{3,515},{515,3},{4... | collective-permute-start | bytes 276488 | tf_op jit(solution)/shard_map/cond/branch_0_fun/ppermute | solution.py:21
  144.8 7.3 %collective-permute-done.21 = bf16[2,72,320]{2,1,0:T(8,128)(2,1)S(1)} collective-permute-done((bf16[2,72,320]{2,1,0:T(8,128)(2,1)S(1)}, bf16[2,72,320]{2,1,0:T(8,128)(2,1)S(1)}, u32[]{:S(2)}, u32[]{:S(2)}) %collective-permute-start.21) | collective-permute-done | bytes 92192 | tf_op jit(solution)/shard_map/cond/branch_0_fun/ppermute | solution.py:21
  152.1 7.9 %collective-permute-start.23 = (f32[72,320]{1,0:T(8,128)S(1)}, f32[72,320]{1,0:T(8,128)S(1)}, u32[]{:S(2)}, u32[]{:S(2)}) collective-permute-start(f32[72,320]{1,0:T(8,128)S(1)} %select_bitcast_fusion), channel_id=1, source_target_pairs={{0,8},{8,0},{1,9},{9,1},{2,10},{10,2},{3,11},{11,3},{4,12},{12,4},... | collective-permute-start | bytes 276488 | tf_op jit(solution)/shard_map/cond/branch_0_fun/ppermute | solution.py:21
  160.0 0.0 all-to-all-done.17
  160.0 2.9 %collective-permute-start.22 = (bf16[768,128]{1,0:T(8,128)(2,1)S(1)}, bf16[768,128]{1,0:T(8,128)(2,1)S(1)}, u32[]{:S(2)}, u32[]{:S(2)}) collective-permute-start(bf16[768,128]{1,0:T(8,128)(2,1)S(1)} %bitcast.118), channel_id=1, source_target_pairs={{0,8},{8,0},{1,9},{9,1},{2,10},{10,2},{3,11},{11,3},{4,12},{12,4},... | collective-permute-start | bytes 589832 | tf_op jit(solution)/shard_map/cond/branch_0_fun/ppermute | solution.py:21
  163.0 0.0 collective-permute-done.23
  163.0 0.7 maximum_bitcast_fusion
  163.7 0.3 collective-permute-done.22.other_ref
  164.0 1.4 unpacked.5
  (12 shorter events, 0.3 us)
Async XLA Ops:
  5.6 6.0 %copy-start.11 = (bf16[320,144]{0,1:T(8,128)(2,1)S(1)}, bf16[320,144]{0,1:T(8,128)(2,1)}, u32[]{:S(2)}) copy-start(bf16[320,144]{0,1:T(8,128)(2,1)} %get-tuple-element.65) | copy-start | bytes 276484 | tf_op jit(solution)/shard_map/cond
  5.6 41.2 %all-to-all-start.12 = ((f32[8,72,640]{2,1,0:T(8,128)}), f32[8,72,640]{2,1,0:T(8,128)S(1)}, u32[]{:S(2)}, u32[]{:S(2)}) async-start(f32[8,72,640]{2,1,0:T(8,128)} %broadcast_in_dim.26), calls=%async_computation.12 | async-start | bytes 2949120 | tf_op jit(solution)/shard_map/cond/branch_0_fun/all_to_all | solution.py:25
  11.7 5.9 %collective-permute-start.16 = (bf16[72,640]{1,0:T(8,128)(2,1)S(1)}, bf16[72,640]{1,0:T(8,128)(2,1)S(1)}, u32[]{:S(2)}, u32[]{:S(2)}) collective-permute-start(bf16[72,640]{1,0:T(8,128)(2,1)S(1)} %pad_maximum_fusion.4), channel_id=1, source_target_pairs={{0,16},{16,0},{1,17},{17,1},{2,18},{18,2},{3,19},{19,3},{4,20},{20... | collective-permute-start | bytes 276488 | tf_op jit(solution)/shard_map/cond/branch_0_fun/ppermute | solution.py:21
  17.7 18.1 %collective-permute-start.17 = (bf16[2,72,640]{2,1,0:T(8,128)(2,1)S(1)}, bf16[2,72,640]{2,1,0:T(8,128)(2,1)S(1)}, u32[]{:S(2)}, u32[]{:S(2)}) collective-permute-start(bf16[2,72,640]{2,1,0:T(8,128)(2,1)S(1)} %pad_maximum_fusion.3), channel_id=1, source_target_pairs={{0,512},{512,0},{1,513},{513,1},{2,514},{514,2},{3,515},{515,3},{4... | collective-permute-start | bytes 552968 | tf_op jit(solution)/shard_map/cond/branch_0_fun/ppermute | solution.py:21
  35.8 27.5 %copy-start.18 = (s32[1,320]{1,0:T(1,128)S(1)}, s32[1,320]{1,0:T(1,128)}, u32[]{:S(2)}) copy-start(s32[1,320]{1,0:T(1,128)} %get-tuple-element.62.label_ref) | copy-start | bytes 3844 | tf_op jit(solution)/shard_map/cond
  35.8 10.0 %collective-permute-start.18 = (bf16[4,72,640]{2,1,0:T(8,128)(2,1)S(1)}, bf16[4,72,640]{2,1,0:T(8,128)(2,1)S(1)}, u32[]{:S(2)}, u32[]{:S(2)}) collective-permute-start(bf16[4,72,640]{2,1,0:T(8,128)(2,1)S(1)} %pad_maximum_fusion.1), channel_id=1, source_target_pairs={{0,8},{8,0},{1,9},{9,1},{2,10},{10,2},{3,11},{11,3},{4,12},{12,4},... | collective-permute-start | bytes 1105928 | tf_op jit(solution)/shard_map/cond/branch_0_fun/ppermute | solution.py:21
  46.8 16.5 %all-to-all-start.13 = ((bf16[8,72,640]{2,1,0:T(8,128)(2,1)}), bf16[8,72,640]{2,1,0:T(8,128)(2,1)S(1)}, u32[]{:S(2)}, u32[]{:S(2)}) async-start(bf16[8,72,640]{2,1,0:T(8,128)(2,1)} %pad_maximum_fusion), calls=%async_computation.13 | async-start | bytes 1474560 | tf_op jit(solution)/shard_map/cond/branch_0_fun/all_to_all | solution.py:25
  51.7 15.4 %collective-permute-start.19 = (bf16[320,1152]{1,0:T(8,128)(2,1)}, bf16[320,1152]{1,0:T(8,128)(2,1)S(1)}, u32[]{:S(2)}, u32[]{:S(2)}) collective-permute-start(bf16[320,1152]{1,0:T(8,128)(2,1)} %get-tuple-element.64.feats_ref), channel_id=1, source_target_pairs={{0,8},{8,0},{1,9},{9,1},{2,10},{10,2},{3,11},{11,3},{4,12},{12,4},... | collective-permute-start | bytes 2211848 | tf_op jit(solution)/shard_map/cond/branch_0_fun/ppermute | solution.py:21
  67.1 23.7 %copy-start.6 = (bf16[320,1152]{1,0:T(8,128)(2,1)S(1)}, bf16[320,1152]{1,0:T(8,128)(2,1)}, u32[]{:S(2)}) copy-start(bf16[320,1152]{1,0:T(8,128)(2,1)} %get-tuple-element.64.feats_ref) | copy-start | bytes 2211844 | tf_op jit(solution)/shard_map/cond
  92.6 30.7 %all-to-all-start.15 = ((bf16[16,48,128]{2,1,0:T(8,128)(2,1)}), bf16[16,48,128]{2,1,0:T(8,128)(2,1)S(1)}, u32[]{:S(2)}, u32[]{:S(2)}) async-start(bf16[16,48,128]{2,1,0:T(8,128)(2,1)} %bitcast.7), calls=%async_computation.15 | async-start | bytes 393216 | tf_op jit(solution)/shard_map/cond/branch_0_fun/all_to_all | solution.py:25
  110.9 16.3 %collective-permute-start.20 = (bf16[2,2,72,320]{3,2,1,0:T(8,128)(2,1)S(1)}, bf16[2,2,72,320]{3,2,1,0:T(8,128)(2,1)S(1)}, u32[]{:S(2)}, u32[]{:S(2)}) collective-permute-start(bf16[2,2,72,320]{3,2,1,0:T(8,128)(2,1)S(1)} %get-tuple-element.69), channel_id=1, source_target_pairs={{0,16},{16,0},{1,17},{17,1},{2,18},{18,2},{3,19},{19,3},{4,20},{20... | collective-permute-start | bytes 552968 | tf_op jit(solution)/shard_map/cond/branch_0_fun/ppermute | solution.py:21
  124.0 10.6 %all-to-all-start.16 = ((f32[4,48,128]{2,1,0:T(8,128)}), f32[4,48,128]{2,1,0:T(8,128)S(1)}, u32[]{:S(2)}, u32[]{:S(2)}) async-start(f32[4,48,128]{2,1,0:T(8,128)} %broadcast_in_dim.27), calls=%async_computation.16 | async-start | bytes 196608 | tf_op jit(solution)/shard_map/cond/branch_0_fun/all_to_all | solution.py:25
  135.3 24.8 %all-to-all-start.17 = ((bf16[16,48,128]{2,1,0:T(8,128)(2,1)}), bf16[16,48,128]{2,1,0:T(8,128)(2,1)S(1)}, u32[]{:S(2)}, u32[]{:S(2)}) async-start(bf16[16,48,128]{2,1,0:T(8,128)(2,1)} %broadcast_in_dim.32), calls=%async_computation.17 | async-start | bytes 393216 | tf_op jit(solution)/shard_map/cond/branch_0_fun/all_to_all | solution.py:25
  142.6 9.5 %collective-permute-start.21 = (bf16[2,72,320]{2,1,0:T(8,128)(2,1)S(1)}, bf16[2,72,320]{2,1,0:T(8,128)(2,1)S(1)}, u32[]{:S(2)}, u32[]{:S(2)}) collective-permute-start(bf16[2,72,320]{2,1,0:T(8,128)(2,1)S(1)} %fusion.1), channel_id=1, source_target_pairs={{0,512},{512,0},{1,513},{513,1},{2,514},{514,2},{3,515},{515,3},{4... | collective-permute-start | bytes 276488 | tf_op jit(solution)/shard_map/cond/branch_0_fun/ppermute | solution.py:21
  152.1 10.9 %collective-permute-start.23 = (f32[72,320]{1,0:T(8,128)S(1)}, f32[72,320]{1,0:T(8,128)S(1)}, u32[]{:S(2)}, u32[]{:S(2)}) collective-permute-start(f32[72,320]{1,0:T(8,128)S(1)} %select_bitcast_fusion), channel_id=1, source_target_pairs={{0,8},{8,0},{1,9},{9,1},{2,10},{10,2},{3,11},{11,3},{4,12},{12,4},... | collective-permute-start | bytes 276488 | tf_op jit(solution)/shard_map/cond/branch_0_fun/ppermute | solution.py:21
  160.0 4.0 %collective-permute-start.22 = (bf16[768,128]{1,0:T(8,128)(2,1)S(1)}, bf16[768,128]{1,0:T(8,128)(2,1)S(1)}, u32[]{:S(2)}, u32[]{:S(2)}) collective-permute-start(bf16[768,128]{1,0:T(8,128)(2,1)S(1)} %bitcast.118), channel_id=1, source_target_pairs={{0,8},{8,0},{1,9},{9,1},{2,10},{10,2},{3,11},{11,3},{4,12},{12,4},... | collective-permute-start | bytes 589832 | tf_op jit(solution)/shard_map/cond/branch_0_fun/ppermute | solution.py:21
